TPU v7x, 32 devices: a whole 2x2x4 slice. The times are simulated.
32 devices in a mesh: ctx: 8 (over y, x, core), ch: 4 (over z).
Axes of the slice: x: 2, y: 2, z: 4, core: 2. Of those that a mesh axis runs over, the one named last changes fastest.
Arguments:
- query_proj: bfloat16 [2048, 4096], P('ctx', 'ch'), may hold values from -6 to 6
- key_proj: bfloat16 [2048, 4096], P('ctx', 'ch'), may hold values from -6 to 6
- value_proj: bfloat16 [2048, 4096], P('ctx', 'ch'), may hold values from -6 to 6
- filter_in: float32 [33, 64], replicated, may hold values from -3 to 3
- filter_bias: float32 [64], replicated, may hold values from -3.140625 to 3.140625
- filter_out: float32 [64, 256], P(None, 'ch'), may hold values from -0.015625 to 0.015625
- decay_rates: float32 [256], P('ch'), may hold values from 9.765625e-05 to 0.0333333333
- skip_gain: float32 [4096], P('ch'), may hold values from -4 to 4
- out_weight: bfloat16 [4096, 4096], P('ch', 'ctx'), may hold values from -0.125 to 0.125
Outputs:
- layer_out: bfloat16 [2048, 4096], P('ctx', 'ch')
All inputs are finite; a program needn't handle non-finite values.
Results may differ from a plain program's by a relative error of at most 0.012.
Values may be sent and summed in bfloat16 or wider, within the bound.
No kernel may reach another device: no remote copies, remote signals or barrier semaphores. Data moves between devices by JAX's collectives and lax.ppermute only.
A program may use at most 128 MiB of HBM per device.

v0:
```python
import math

import jax
import jax.numpy as jnp
from jax import lax
from jax.sharding import PartitionSpec as P


def position_features(lag_index, seq_len, band_count):
    clamped = jnp.maximum(lag_index, 0)
    harmonics = jnp.arange(1, band_count + 1, dtype=jnp.int32)
    phases = (clamped[:, None] * harmonics[None, :] % seq_len).astype(jnp.float32) * (
        2.0 * math.pi / seq_len
    )
    ramp_term = (clamped.astype(jnp.float32) / seq_len)[:, None]
    return jnp.concatenate([ramp_term, jnp.cos(phases), jnp.sin(phases)], axis=1)


def filter_values(lag_index, seq_len, filter_in, filter_bias, filter_out, decay_rates):
    band_count = (filter_in.shape[0] - 1) // 2
    features = position_features(lag_index, seq_len, band_count)
    hidden = jnp.sin(
        jnp.dot(
            features, filter_in, precision=lax.Precision.HIGHEST, preferred_element_type=jnp.float32
        )
        + filter_bias
    )
    raw_values = jnp.dot(
        hidden, filter_out, precision=lax.Precision.HIGHEST, preferred_element_type=jnp.float32
    )
    clamped = jnp.maximum(lag_index, 0).astype(jnp.float32)
    shaped = raw_values * jnp.exp(-decay_rates[None, :] * clamped[:, None])
    return jnp.where((lag_index >= 0)[:, None], shaped, jnp.zeros((), jnp.float32)).astype(
        jnp.bfloat16
    )


def toeplitz(values, out_rows, in_rows):
    rows_idx = jnp.arange(out_rows, dtype=jnp.int32)
    cols_idx = jnp.arange(in_rows, dtype=jnp.int32)
    positions = in_rows - 1 + rows_idx[:, None] - cols_idx[None, :]
    return jnp.take(values, positions, axis=1)


def local(
    query_proj,
    key_proj,
    value_proj,
    filter_in,
    filter_bias,
    filter_out,
    decay_rates,
    skip_gain,
    out_weight,
):
    ctx_count = lax.axis_size("ctx")
    local_rows = query_proj.shape[0]
    channels = query_proj.shape[1]
    seq_len = local_rows * ctx_count
    groups_dev = filter_out.shape[1]
    group_width = channels // groups_dev
    own_index = lax.axis_index("ctx")
    conv_input = (key_proj.astype(jnp.float32) * value_proj.astype(jnp.float32)).astype(
        jnp.bfloat16
    )
    own_start = own_index * local_rows
    piece = lax.all_gather(conv_input, "ctx", axis=0, tiled=True)
    piece_rows = piece.shape[0]
    sub_rows = math.gcd(piece_rows, local_rows)
    sub_count = piece_rows // sub_rows

    def one_sub(step, current):
        sub_start = step * sub_rows

        def accumulate(inner):
            source = lax.dynamic_slice_in_dim(piece, step * sub_rows, sub_rows, 0)
            lag_index = (
                own_start
                - sub_start
                - (sub_rows - 1)
                + jnp.arange(local_rows + sub_rows - 1, dtype=jnp.int32)
            )
            group_filters = filter_values(
                lag_index, seq_len, filter_in, filter_bias, filter_out, decay_rates
            )
            toeplitz_tile = toeplitz(group_filters.T, local_rows, sub_rows)
            product = jnp.einsum(
                "gts,sgj->tgj",
                toeplitz_tile,
                source.reshape(sub_rows, groups_dev, group_width),
                preferred_element_type=jnp.float32,
            )
            return inner + product.reshape(local_rows, channels)

        return lax.cond(sub_start >= own_start + local_rows, lambda kept: kept, accumulate, current)

    convolved = lax.fori_loop(0, sub_count, one_sub, jnp.zeros((local_rows, channels), jnp.float32))
    gated_out = (
        query_proj.astype(jnp.float32)
        * (convolved + skip_gain[None, :] * conv_input.astype(jnp.float32))
    ).astype(jnp.bfloat16)
    partial_terms = jnp.dot(
        gated_out,
        lax.all_gather(out_weight, "ctx", axis=1, tiled=True),
        preferred_element_type=jnp.float32,
    )
    return lax.psum_scatter(
        partial_terms.astype(jnp.bfloat16), "ch", scatter_dimension=1, tiled=True
    )


def solution(mesh):
    placed = (
        P("ctx", "ch"),
        P("ctx", "ch"),
        P("ctx", "ch"),
        P(),
        P(),
        P(None, "ch"),
        P("ch"),
        P("ch"),
        P("ch", "ctx"),
    )
    return jax.shard_map(
        local, mesh=mesh, in_specs=placed, out_specs=P("ctx", "ch"), check_vma=False
    )
```

profile of v0, /device:TPU:0, one launch (start us, length us, event | category | flops | bytes accessed | tf_op | source)
XLA Modules:
  0.0 2179.8 jit_solution(5313386042862752780)
XLA Ops:
  6.5 0.0 all-gather.3.cloned.1.call-start
  6.5 1.2 copy.23
  7.8 1.2 copy.24
  9.0 0.9 multiply_convert_fusion.1
  10.0 0.0 all-gather.3.cloned.1.call-update
  10.0 0.0 all-gather.5.cloned.1.call-start
  10.0 0.7 all-gather.5.cloned.1.call-update
  10.7 0.0 reduce-scatter.2.cloned.1.call-start
  10.8 2.0 copy.22
  12.8 37.4 %all-gather.3.cloned.1.call-done = bf16[2048,1024]{0,1:T(8,128)(2,1)} async-done(((bf16[256,1024]{0,1:T(8,128)(2,1)}), bf16[2048,1024]{0,1:T(8,128)(2,1)}) %all-gather.3.cloned.1.call-update) | async-done | bytes 4194320 | tf_op jit(solution)/shard_map/all_gather | solution.py:67
  50.3 0.1 broadcast_in_dim.33
  50.3 0.0 copy-start
  50.4 0.0 copy-start.1
  50.4 0.0 copy-start.2
  50.4 259.3 %while.17 = (s32[]{:T(128)}, f32[256,1024]{0,1:T(8,128)S(1)}, s32[]{:T(128)}, bf16[2048,1024]{0,1:T(8,128)(2,1)}, s32[]{:T(128)}, /*index=5*/f32[33,64]{1,0:T(8,...) while((s32[]{:T(128)}, f32[256,1024]{0,1:T(8,128)S(1)}, s32[]{:T(128)}, ...), condition=%wide.region_3.4_spmd, body=%wide.region_0.3_spmd.sunk | while | flops 177844720 | bytes 50045456 | solution.py:97
  50.4 258.9 %conditional.2 = (f32[256,1024]{0,1:T(8,128)S(1)}) conditional(s32[]{:T(128)} %convert_element_type.80, (s32[]{:T(128)}, bf16[2048,1024]{0,1:T(8,128)(2,1)}, s32[]{:T(128)}, s32[]{:T(128)}, f32[33,64]{1,0:T(8,128)}, /*index=5*/f32[64]{0:T(128)}, f32[64,64]{1,0:T(8,128)}, f32[64]{0:T(128)}, f32[256,1024]{0,1:T(8,128)S(1)}) %tuple.46, ...), branch_computations={%region_1.1_spmd, %region_2.2_spmd} | conditional | flops 177844720 | bytes 50045252 | solution.py:95
  50.4 0.2 fusion.22
  50.7 1.5 fusion.7
  52.2 0.7 neg.3
  52.8 1.1 fusion.8
  53.9 0.1 copy.20
  54.0 0.1 fusion.9
  54.2 0.1 copy.25
  54.3 229.0 %gather_fusion = bf16[65536,64]{1,0:T(8,128)(2,1)} fusion(bf16[64,511]{0,1:T(8,128)(2,1)S(1)} %copy.20, s32[65536]{0:T(1024)S(1)} %broadcast_clamp_fusion), kind=kCustom, calls=%fused_computation | custom fusion | bytes 17039360 | tf_op jit(solution)/shard_map/while/body/eval_jaxpr/cond/branch_0_fun/jit(_take)/gather | solution.py:42
  283.3 18.9 copy.21
  302.2 1.1 constant_dynamic-slice_fusion
  303.3 0.2 fusion.12
  303.4 5.7 fusion
  309.1 0.2 bitcast_add_fusion
  309.6 0.0 all-gather.5.cloned.1.call-done
  309.7 0.0 copy-done
  309.7 0.0 copy-done.1
  309.7 0.0 copy-done.2
  309.7 7.2 convolution_convert_fusion
  316.9 0.0 reduce-scatter.2.cloned.1.call-update
  317.0 1856.3 %reduce-scatter.2.cloned.1.call-done = bf16[256,1024]{1,0:T(8,128)(2,1)} async-done(((bf16[256,4096]{1,0:T(8,128)(2,1)}), bf16[256,1024]{1,0:T(8,128)(2,1)}) %reduce-scatter.2.cloned.1.call-update) | async-done | bytes 524304 | tf_op jit(solution)/shard_map/reduce_scatter | solution.py:107
  (13 shorter events, 0.1 us)
Async XLA Ops:
  6.5 43.7 %all-gather.3.cloned.1.call-start = ((), (), s32[]{:S(2)}) async-start(), calls=%async_computation.1 | async-start | bytes 4718592 | tf_op jit(solution)/shard_map/all_gather | solution.py:67
  10.0 299.7 %all-gather.5.cloned.1.call-start = ((), (), s32[]{:S(2)}) async-start(), calls=%async_computation.2 | async-start | bytes 9437184 | tf_op jit(solution)/shard_map/all_gather | solution.py:104
  10.7 2162.5 %reduce-scatter.2.cloned.1.call-start = ((), (), s32[]{:S(2)}) async-start(), calls=%async_computation.3 | async-start | bytes 2621440 | tf_op jit(solution)/shard_map/reduce_scatter | solution.py:107
  50.3 259.3 %copy-start = (bf16[256,1024]{0,1:T(8,128)(2,1)S(1)}, bf16[256,1024]{0,1:T(8,128)(2,1)}, u32[]{:S(2)}) copy-start(bf16[256,1024]{0,1:T(8,128)(2,1)} %multiply_convert_fusion.1) | copy-start | bytes 1572868
  50.4 259.3 %copy-start.1 = (bf16[256,1024]{0,1:T(8,128)(2,1)S(1)}, bf16[256,1024]{0,1:T(8,128)(2,1)}, u32[]{:S(2)}) copy-start(bf16[256,1024]{0,1:T(8,128)(2,1)} %copy.22) | copy-start | bytes 1572868
  50.4 259.3 %copy-start.2 = (f32[1024]{0:T(1024)S(1)}, f32[1024]{0:T(1024)}, u32[]{:S(2)}) copy-start(f32[1024]{0:T(1024)} %param.20) | copy-start | bytes 12292
Sparse Core Ops, SparseCore 0:
  10.1 40.1 all-gather.2
  52.1 55.9 all-gather.4
  317.1 1856.0 reduce-scatter.1
where the time goes:
time: 2190 us; the launch traced here: 2180 us
  waiting for transfers between devices  1890 us (86%)
  local copies, waits for them, and re-layouts  254 us (12%)
    reduce_scatter x1, waiting for transfers between devices, local(): lax.psum_scatter(partial_terms.astype(jnp.bfloat16), 'ch', scatter_dimens...  1860 us
    gather x2, local copies, waits for them, and re-layouts, toeplitz(): return jnp.take(values, positions, axis=1)  248 us
  transfers between devices with their start and end apart: 3, of which 2 were waited for; matrix products, arithmetic and copies ran while one was open for 12% of the time, Pallas kernels for 0%

commit v1 on v0

v1 whole, which is shorter than its diff:
```python
import functools
import math

import jax
import jax.numpy as jnp
from jax import lax
from jax.experimental import pallas as pl
from jax.experimental.pallas import tpu as pltpu
from jax.sharding import PartitionSpec as P

BF = jnp.bfloat16
F32 = jnp.float32
LANE = 128
SUB = 16
PARAMS = pltpu.CompilerParams(vmem_limit_bytes=48 * 1024 * 1024)


def pre_kernel(k_ref, v_ref, o_ref):
    prod = k_ref[...].astype(F32) * v_ref[...].astype(F32)
    o_ref[...] = prod.T.astype(BF)


def taps_kernel(seq, me_ref, fin_ref, bias_ref, fout_ref, decay_ref, o_ref):
    bands = (fin_ref.shape[0] - 1) // 2
    groups = o_ref.shape[0]
    all_groups = fout_ref.shape[1]
    contract = functools.partial(
        lax.dot_general, precision=lax.Precision.HIGHEST, preferred_element_type=F32
    )
    first = (((0,), (0,)), ((), ()))
    harmonic = lax.broadcasted_iota(jnp.int32, (bands, seq), 0) + 1
    lag = lax.broadcasted_iota(jnp.int32, (bands, seq), 1)
    phase = lax.rem(harmonic * lag, seq).astype(F32) * (2.0 * math.pi / seq)
    time = lax.broadcasted_iota(jnp.int32, (1, seq), 1).astype(F32)
    pre = contract(fin_ref[1 : 1 + bands, :], jnp.cos(phase), first)
    pre += contract(fin_ref[1 + bands : 1 + 2 * bands, :], jnp.sin(phase), first)
    pre += contract(fin_ref[0:1, :], time / seq, first)
    pre += contract(bias_ref[...], jnp.ones((1, seq), F32), first)
    hidden = jnp.sin(pre)
    row = lax.broadcasted_iota(jnp.int32, (groups, all_groups), 0)
    col = lax.broadcasted_iota(jnp.int32, (groups, all_groups), 1)
    pick = (col == me_ref[0] * groups + row).astype(F32)
    fout = contract(pick, fout_ref[...], (((1,), (1,)), ((), ())))
    decay = jnp.sum(pick * decay_ref[...], axis=1, keepdims=True)
    raw = contract(fout, hidden, (((1,), (0,)), ((), ())))
    o_ref[:, :LANE] = jnp.zeros((groups, LANE), F32)
    o_ref[:, LANE:] = (raw * jnp.exp(-decay * time)).astype(BF).astype(F32)


def conv_kernel(seq, width, taps_ref, u_ref, o_ref, toep, lhs):
    blocks = seq // LANE
    per = u_ref.shape[2] // LANE
    groups = taps_ref.shape[0]
    lhs[...] = jnp.zeros_like(lhs)

    def one(g, carry):
        at = pl.multiple_of(g * width, width)
        line = jnp.broadcast_to(taps_ref[pl.ds(g, 1), :], (SUB, LANE + seq))
        slab = pltpu.roll(line, 0, 1, stride=1, stride_axis=0)
        for k in range(LANE // SUB):
            part = (slab if k == 0 else pltpu.roll(slab, SUB * k, 1)).astype(BF)
            for d in range(blocks):
                toep[LANE * d + SUB * k : LANE * d + SUB * (k + 1), :] = part[
                    :, LANE * (d + 1) : LANE * (d + 2)
                ]
        for b in range(blocks):
            for d in range(b + 1):
                a = b - d
                lhs[width * b : width * (b + 1), LANE * d : LANE * (d + 1)] = u_ref[
                    a // per, pl.ds(at, width), LANE * (a % per) : LANE * (a % per + 1)
                ]
        out = jnp.dot(lhs[...], toep[...], preferred_element_type=F32).astype(BF)
        for b in range(blocks):
            o_ref[b // per, pl.ds(at, width), LANE * (b % per) : LANE * (b % per + 1)] = out[
                width * b : width * (b + 1), :
            ]
        return carry

    lax.fori_loop(0, groups, one, 0)


def gate_kernel(q_ref, k_ref, v_ref, skip_ref, conv_ref, o_ref):
    u = (k_ref[...].astype(F32) * v_ref[...].astype(F32)).astype(BF).astype(F32)
    conv = conv_ref[...].astype(F32).T
    o_ref[...] = (q_ref[...].astype(F32) * (conv + skip_ref[...] * u)).astype(BF)


def project_kernel(sets, ctx_count, ch_count, place_ref, x_ref, *refs):
    weights, (keep_ref, send_ref) = refs[:-2], refs[-2:]
    me, z = place_ref[0], place_ref[1]
    share = ctx_count // ch_count
    for rel in range(ctx_count):
        total = None
        for ref, part in zip(weights, sets):
            for slot, (offset, start, size) in enumerate(part):
                if offset == rel:
                    term = jnp.dot(
                        x_ref[:, start : start + size],
                        ref[slot],
                        preferred_element_type=F32,
                    )
                    total = term if total is None else total + term
        total = total.astype(BF)
        owner = jnp.bitwise_xor(me, rel)
        r = jnp.bitwise_xor(owner // share, z)
        h = owner % share

        @pl.when(r % 2 == 0)
        def _():
            keep_ref[r // 2, h] = total

        @pl.when(r % 2 == 1)
        def _():
            send_ref[r // 2, h] = total


def swap(value, axis, bit):
    count = lax.axis_size(axis)
    return lax.ppermute(value, axis, [(i, i ^ bit) for i in range(count)])


def gather_half(piece, start, bits):
    held = piece[None]
    note = [(0, start, piece.shape[0])]
    for bit in bits[:-1]:
        held = jnp.concatenate([held, swap(held, "ctx", bit)], 0)
        note = note + [(o ^ bit, s, n) for o, s, n in note]
    last = bits[-1]
    return [(held, note), (swap(held, "ctx", last), [(o ^ last, s, n) for o, s, n in note])]


def local(
    query_proj,
    key_proj,
    value_proj,
    filter_in,
    filter_bias,
    filter_out,
    decay_rates,
    skip_gain,
    out_weight,
):
    ctx_count = lax.axis_size("ctx")
    ch_count = lax.axis_size("ch")
    rows, channels = query_proj.shape
    seq = rows * ctx_count
    groups_dev = filter_out.shape[1]
    width = channels // groups_dev
    own = channels // ctx_count
    depth, columns = out_weight.shape
    me = lax.axis_index("ctx")
    z = lax.axis_index("ch")
    place = jnp.stack([me, z]).astype(jnp.int32)
    smem = pl.BlockSpec(memory_space=pltpu.SMEM)
    vmem = pl.BlockSpec(memory_space=pltpu.VMEM)

    u_t = pl.pallas_call(
        pre_kernel,
        out_shape=jax.ShapeDtypeStruct((channels, rows), BF),
        compiler_params=PARAMS,
    )(key_proj, value_proj)
    taps = pl.pallas_call(
        functools.partial(taps_kernel, seq),
        out_shape=jax.ShapeDtypeStruct((own // width, LANE + seq), F32),
        in_specs=[smem] + [vmem] * 4,
        compiler_params=PARAMS,
    )(place, filter_in, filter_bias[None], filter_out, decay_rates[None])
    u_all = lax.all_to_all(u_t.reshape(ctx_count, own, rows), "ctx", 0, 0)
    conv_all = pl.pallas_call(
        functools.partial(conv_kernel, seq, width),
        out_shape=jax.ShapeDtypeStruct(u_all.shape, BF),
        scratch_shapes=[
            pltpu.VMEM((seq, LANE), BF),
            pltpu.VMEM((seq // LANE * width, seq), BF),
        ],
        compiler_params=PARAMS,
    )(taps, u_all)
    conv_t = lax.all_to_all(conv_all, "ctx", 0, 0).reshape(channels, rows)
    gated = pl.pallas_call(
        gate_kernel,
        out_shape=jax.ShapeDtypeStruct((rows, channels), BF),
        compiler_params=PARAMS,
    )(query_proj, key_proj, value_proj, skip_gain[None], conv_t)

    bits = [1 << i for i in range(1, ctx_count.bit_length() - 1)]
    chunk = max(LANE, columns // 2)
    share = ctx_count // ch_count
    results = []
    for at in range(0, columns, chunk):
        part = out_weight[:, at : at + chunk]
        half = depth // 2
        held = gather_half(part[:half], 0, bits + [1]) + gather_half(
            part[half:], half, bits[::-1] + [1]
        )
        keep, send = pl.pallas_call(
            functools.partial(project_kernel, [n for _, n in held], ctx_count, ch_count),
            out_shape=[jax.ShapeDtypeStruct((ch_count // 2, share, rows, chunk), BF)] * 2,
            in_specs=[smem] + [vmem] * (1 + len(held)),
            compiler_params=PARAMS,
        )(place, gated, *[w for w, _ in held])
        bit = 1
        while True:
            got = swap(send, "ch", bit)
            total = keep.astype(F32) + got.astype(F32)
            bit *= 2
            if bit == ch_count:
                break
            keep, send = total[0::2], total[1::2].astype(BF)
        results.append(total[0].astype(BF))
    whole = jnp.stack(results, 0)
    return whole.transpose(2, 1, 0, 3).reshape(rows, share * columns)


def solution(mesh):
    placed = (
        P("ctx", "ch"),
        P("ctx", "ch"),
        P("ctx", "ch"),
        P(),
        P(),
        P(None, "ch"),
        P("ch"),
        P("ch"),
        P("ch", "ctx"),
    )
    return jax.shard_map(
        local, mesh=mesh, in_specs=placed, out_specs=P("ctx", "ch"), check_vma=False
    )
```

time: 2190 us -> 124 us (0.06)
  waiting for transfers between devices: 1890 us -> 56.1 us
  local copies, waits for them, and re-layouts: 254 us -> 3.24 us
  Pallas kernels: 0 us -> 23.8 us
    reduce_scatter x1 -> x0, waiting for transfers between devices: 1860 us -> none  [local(): lax.psum_scatter(partial_terms.astype(jnp.bfloat16), 'ch', scatter_dimens...]
    gather x2 -> x0, local copies, waits for them, and re-layouts: 248 us -> none  [toeplitz(): return jnp.take(values, positions, axis=1)]
    ppermute x0 -> x16, waiting for transfers between devices: none -> 56.1 us  [swap(): return lax.ppermute(value, axis, [(i, i ^ bit) for i in range(count)])]
    all_gather x2 -> x0, waiting for transfers between devices: 37.5 us -> none  [the longest x1 37.4 us: local(): piece = lax.all_gather(conv_input, 'ctx', axis=0, tiled=True)]
    pallas_call x0 -> x6, Pallas kernels: none -> 23.8 us  [the longest x2 10.3 us: local(): pl.pallas_call(functools.partial(project_kernel, [n for _, n in held], ct...]
  transfers between devices with their start and end apart: 3 -> 17, of which waited for: 2 -> 9; matrix products, arithmetic and copies ran while one was open for 12% -> 6% of each run, Pallas kernels for 0% -> 19%
where the time goes in v1:
time: 124 us; the launch traced here: 123 us
  waiting for transfers between devices  56.1 us (45%)
  Pallas kernels  23.8 us (19%)
  starting transfers between devices  20.8 us (17%)
  blocking collectives  12.4 us (10%)
  other arithmetic  6.86 us (6%)
  local copies, waits for them, and re-layouts  3.24 us (3%)
    ppermute x16, waiting for transfers between devices, swap(): return lax.ppermute(value, axis, [(i, i ^ bit) for i in range(count)])  56.1 us
    ppermute x16, starting transfers between devices, swap(): return lax.ppermute(value, axis, [(i, i ^ bit) for i in range(count)])  16.6 us
    all_to_all x1, blocking collectives, local(): conv_t = lax.all_to_all(conv_all, 'ctx', 0, 0).reshape(channels, rows)  12.4 us
    pallas_call x2, Pallas kernels, local(): pl.pallas_call(functools.partial(project_kernel, [n for _, n in held], ct...  10.3 us
    pallas_call x1, Pallas kernels, local(): pl.pallas_call(functools.partial(conv_kernel, seq, width), out_shape=jax....  7.9 us
    concatenate x8, other arithmetic, gather_half(): held = jnp.concatenate([held, swap(held, 'ctx', bit)], 0)  6.38 us
    all_to_all x1, starting transfers between devices, local(): u_all = lax.all_to_all(u_t.reshape(ctx_count, own, rows), 'ctx', 0, 0)  4.16 us
    pallas_call x1, Pallas kernels, local(): pl.pallas_call(functools.partial(taps_kernel, seq), out_shape=jax.ShapeDt...  4.15 us
  transfers between devices with their start and end apart: 17, of which 9 were waited for; matrix products, arithmetic and copies ran while one was open for 6% of the time, Pallas kernels for 19%

profile of v1, /device:TPU:0, one launch (start us, length us, event | category | flops | bytes accessed | tf_op | source)
XLA Modules:
  0.0 123.4 jit_solution(223308295074952148)
XLA Ops:
  0.0 1.3 %slice_bitcast_fusion.2 = (bf16[1,512,256]{2,1,0:T(8,128)(2,1)S(1)}, bf16[1,512,256]{2,1,0:T(8,128)(2,1)S(1)}, bf16[1,512,256]{2,1,0:T(8,128)(2,1)S(1)}, bf16[1,512,256]{2,1,0:T(8,128)(2,1)S(1)}) fusion(bf16[1024,512]{1,0:T(8,128)(2,1)} %param.17), kind=kLoop, calls=%fused_computation.19 | loop fusion | bytes 2097152 | tf_op jit(solution)/shard_map/broadcast_in_dim | solution.py:123
  1.3 3.0 %collective-permute-start = (bf16[1,512,256]{2,1,0:T(8,128)(2,1)S(1)}, bf16[1,512,256]{2,1,0:T(8,128)(2,1)S(1)}, u32[]{:S(2)}, u32[]{:S(2)}) collective-permute-start(bf16[1,512,256]{2,1,0:T(8,128)(2,1)S(1)} %get-tuple-element.14), channel_id=1, source_target_pairs={{0,8},{4,12},{8,0},{12,4},{16,24},{20,28},{24,16},{28,20},{1,9},{5... | collective-permute-start | bytes 786440 | tf_op jit(solution)/shard_map/ppermute | solution.py:119
  4.3 1.5 %collective-permute-start.3 = (bf16[1,512,256]{2,1,0:T(8,128)(2,1)S(1)}, bf16[1,512,256]{2,1,0:T(8,128)(2,1)S(1)}, u32[]{:S(2)}, u32[]{:S(2)}) collective-permute-start(bf16[1,512,256]{2,1,0:T(8,128)(2,1)S(1)} %get-tuple-element.13), channel_id=1, source_target_pairs={{0,16},{4,20},{8,24},{12,28},{16,0},{20,4},{24,8},{28,12},{1,17},{... | collective-permute-start | bytes 786440 | tf_op jit(solution)/shard_map/ppermute | solution.py:119
  5.8 0.5 collective-permute-start.11
  6.3 4.3 %collective-permute-done = bf16[1,512,256]{2,1,0:T(8,128)(2,1)S(1)} collective-permute-done((bf16[1,512,256]{2,1,0:T(8,128)(2,1)S(1)}, bf16[1,512,256]{2,1,0:T(8,128)(2,1)S(1)}, u32[]{:S(2)}, u32[]{:S(2)}) %collective-permute-start) | collective-permute-done | bytes 262176 | tf_op jit(solution)/shard_map/ppermute | solution.py:119
  10.6 0.1 pad_maximum_fusion.4
  10.6 1.8 %collective-permute-start.1 = (bf16[2,512,256]{2,1,0:T(8,128)(2,1)S(1)}, bf16[2,512,256]{2,1,0:T(8,128)(2,1)S(1)}, u32[]{:S(2)}, u32[]{:S(2)}) collective-permute-start(bf16[2,512,256]{2,1,0:T(8,128)(2,1)S(1)} %pad_maximum_fusion.4), channel_id=1, source_target_pairs={{0,16},{4,20},{8,24},{12,28},{16,0},{20,4},{24,8},{28,12},{1,17},{... | collective-permute-start | bytes 1572872 | tf_op jit(solution)/shard_map/ppermute | solution.py:119
  12.5 1.5 %collective-permute-start.8 = (bf16[1,512,256]{2,1,0:T(8,128)(2,1)S(1)}, bf16[1,512,256]{2,1,0:T(8,128)(2,1)S(1)}, u32[]{:S(2)}, u32[]{:S(2)}) collective-permute-start(bf16[1,512,256]{2,1,0:T(8,128)(2,1)S(1)} %get-tuple-element.16), channel_id=1, source_target_pairs={{0,8},{4,12},{8,0},{12,4},{16,24},{20,28},{24,16},{28,20},{1,9},{5... | collective-permute-start | bytes 786440 | tf_op jit(solution)/shard_map/ppermute | solution.py:119
  14.0 0.0 collective-permute-done.3
  14.0 0.1 pad_maximum_fusion.5
  14.0 0.6 collective-permute-start.4
  14.6 4.5 %collective-permute-done.11 = bf16[1,512,256]{2,1,0:T(8,128)(2,1)S(1)} collective-permute-done((bf16[1,512,256]{2,1,0:T(8,128)(2,1)S(1)}, bf16[1,512,256]{2,1,0:T(8,128)(2,1)S(1)}, u32[]{:S(2)}, u32[]{:S(2)}) %collective-permute-start.11) | collective-permute-done | bytes 262176 | tf_op jit(solution)/shard_map/ppermute | solution.py:119
  19.1 0.9 pad_maximum_fusion.7
  20.0 0.0 collective-permute-start.12
  20.0 1.7 %collective-permute-done.8 = bf16[1,512,256]{2,1,0:T(8,128)(2,1)S(1)} collective-permute-done((bf16[1,512,256]{2,1,0:T(8,128)(2,1)S(1)}, bf16[1,512,256]{2,1,0:T(8,128)(2,1)S(1)}, u32[]{:S(2)}, u32[]{:S(2)}) %collective-permute-start.8) | collective-permute-done | bytes 262176 | tf_op jit(solution)/shard_map/ppermute | solution.py:119
  21.7 0.9 pad_maximum_fusion.6
  22.6 0.4 collective-permute-start.9
  23.0 1.0 shard_map.92
  24.0 4.2 %all-to-all-start = ((bf16[8,128,256]{2,1,0:T(8,128)(2,1)}), bf16[8,128,256]{2,1,0:T(8,128)(2,1)}, u32[]{:S(2)}, u32[]{:S(2)}) async-start(bf16[8,128,256]{2,1,0:T(8,128)(2,1)} %bitcast.5), calls=%async_computation | async-start | bytes 1048576 | tf_op jit(solution)/shard_map/all_to_all | solution.py:168
  28.1 2.2 %collective-permute-done.1 = bf16[2,512,256]{2,1,0:T(8,128)(2,1)S(1)} collective-permute-done((bf16[2,512,256]{2,1,0:T(8,128)(2,1)S(1)}, bf16[2,512,256]{2,1,0:T(8,128)(2,1)S(1)}, u32[]{:S(2)}, u32[]{:S(2)}) %collective-permute-start.1) | collective-permute-done | bytes 524320 | tf_op jit(solution)/shard_map/ppermute | solution.py:119
  30.4 0.1 pad_maximum_fusion.refs_0_
  30.5 0.1 collective-permute-start.2
  30.6 2.5 %collective-permute-done.4 = bf16[2,512,256]{2,1,0:T(8,128)(2,1)} collective-permute-done((bf16[2,512,256]{2,1,0:T(8,128)(2,1)S(1)}, bf16[2,512,256]{2,1,0:T(8,128)(2,1)}, u32[]{:S(2)}, u32[]{:S(2)}) %collective-permute-start.4) | collective-permute-done | bytes 524320 | tf_op jit(solution)/shard_map/ppermute | solution.py:119
  33.0 1.1 pad_maximum_fusion.1.refs_2_
  34.2 0.1 collective-permute-start.5
  34.3 10.0 %collective-permute-done.12 = bf16[2,512,256]{2,1,0:T(8,128)(2,1)} collective-permute-done((bf16[2,512,256]{2,1,0:T(8,128)(2,1)}, bf16[2,512,256]{2,1,0:T(8,128)(2,1)}, u32[]{:S(2)}, u32[]{:S(2)}) %collective-permute-start.12) | collective-permute-done | bytes 524320 | tf_op jit(solution)/shard_map/ppermute | solution.py:119
  44.3 1.1 pad_maximum_fusion.3.refs_2_
  45.4 0.1 collective-permute-start.13
  45.5 0.0 copy-start.5
  45.6 0.0 copy-start.9
  45.6 2.1 %pad_maximum_fusion.2.refs_0_ = bf16[4,512,256]{2,1,0:T(8,128)(2,1)} fusion(bf16[2,512,256]{2,1,0:T(8,128)(2,1)} %collective-permute-done.9, bf16[1,512,256]{2,1,0:T(8,128)(2,1)S(1)} %copy-done.15, bf16[1,512,256]{2,1,0:T(8,128)(2,1)S(1)} %get-tuple-element.16), kind=kLoop, calls=%fused_computation.2 | loop fusion | flops 1048576 | bytes 2097152 | tf_op jit(solution)/shard_map/concatenate | solution.py:126
  47.7 0.5 collective-permute-start.10
  48.2 0.1 pad_add_fusion.me_ref.place_ref
  48.3 0.2 copy-done.6
  48.4 0.5 copy-done.8
  48.9 4.1 %shard_map.91.taps_ref = f32[8,2176]{1,0:T(8,128)S(1)} custom-call(s32[2]{0:T(128)S(1)} %pad_add_fusion.me_ref.place_ref, f32[33,64]{1,0:T(8,128)S(1)} %copy-done.6, f32[1,64]{1,0:T(1,128)S(1)} %bitcast.20, f32[64,64]{1,0:T(8,128)S(1)} %copy-done.5, f32[1,64]{1,0:T(1,128)S(1)} %bitcast.21), custom_call_target="tpu_custom_call" | custom-call | tf_op jit(solution)/shard_map/pallas_call | solution.py:162
  53.1 0.0 all-to-all-done.u_ref
  53.1 0.0 copy-start.4
  53.1 0.0 copy-start.7
  53.1 7.9 %shard_map.93 = bf16[8,128,256]{2,1,0:T(8,128)(2,1)S(1)} custom-call(f32[8,2176]{1,0:T(8,128)S(1)} %shard_map.91.taps_ref, bf16[8,128,256]{2,1,0:T(8,128)(2,1)} %all-to-all-done.u_ref), custom_call_target="tpu_custom_call" | custom-call | tf_op jit(solution)/shard_map/pallas_call | solution.py:169
  61.0 0.0 copy-start.1
  61.0 0.0 copy-start.3
  61.0 12.4 %all_to_all.10 = bf16[8,128,256]{2,1,0:T(8,128)(2,1)S(1)} all-to-all(bf16[8,128,256]{2,1,0:T(8,128)(2,1)S(1)} %shard_map.93), channel_id=1, replica_groups=mesh['ctx'=8,'ch'=4] {'ctx'}, dimensions={0} | all-to-all | bytes 1048576 | tf_op jit(solution)/shard_map/all_to_all | solution.py:178
  73.5 0.4 shard_map.94.x_ref
  73.9 0.0 collective-permute-done.2.refs_1_
  73.9 5.0 %shard_map.95 = (bf16[2,2,256,256]{3,2,1,0:T(8,128)(2,1)S(1)}, bf16[2,2,256,256]{3,2,1,0:T(8,128)(2,1)S(1)}) custom-call(s32[2]{0:T(128)S(1)} %pad_add_fusion.me_ref.place_ref, bf16[256,1024]{1,0:T(8,128)(2,1)S(1)} %shard_map.94.x_ref, bf16[4,512,256]{2,1,0:T(8,128)(2,1)S(1)} %pad_maximum_fusion.refs_0_, ...), custom_call_target="tpu_custom_call" | custom-call | tf_op jit(solution)/shard_map/pallas_call | solution.py:195
  78.9 1.6 %collective-permute-start.6 = (bf16[2,2,256,256]{3,2,1,0:T(8,128)(2,1)S(1)}, bf16[2,2,256,256]{3,2,1,0:T(8,128)(2,1)S(1)}, u32[]{:S(2)}, u32[]{:S(2)}) collective-permute-start(bf16[2,2,256,256]{3,2,1,0:T(8,128)(2,1)S(1)} %get-tuple-element.10), channel_id=1, source_target_pairs={{0,1},{1,0},{2,3},{3,2},{4,5},{5,4},{6,7},{7,6},{8,9},{9,8},{10,11... | collective-permute-start | bytes 1572872 | tf_op jit(solution)/shard_map/ppermute | solution.py:119
  80.6 0.0 collective-permute-done.13.refs_3_
  80.6 0.0 collective-permute-done.10.refs_1_
  80.6 5.3 %shard_map.96 = (bf16[2,2,256,256]{3,2,1,0:T(8,128)(2,1)S(1)}, bf16[2,2,256,256]{3,2,1,0:T(8,128)(2,1)S(1)}) custom-call(s32[2]{0:T(128)S(1)} %pad_add_fusion.me_ref.place_ref, bf16[256,1024]{1,0:T(8,128)(2,1)S(1)} %shard_map.94.x_ref, bf16[4,512,256]{2,1,0:T(8,128)(2,1)} %pad_maximum_fusion.2.refs_0_, bf16[4,512,256]{2,1,0:T(8,128)(2,1)} %collective-permute-done.10.refs_1_, ...), custom_call_target="tpu_custom_call" | custom-call | tf_op jit(solution)/shard_map/pallas_call | solution.py:195
  85.9 0.5 collective-permute-start.14
  86.4 7.4 %collective-permute-done.6 = bf16[2,2,256,256]{3,2,1,0:T(8,128)(2,1)S(1)} collective-permute-done((bf16[2,2,256,256]{3,2,1,0:T(8,128)(2,1)S(1)}, bf16[2,2,256,256]{3,2,1,0:T(8,128)(2,1)S(1)}, u32[]{:S(2)}, u32[]{:S(2)}) %collective-permute-start.6) | collective-permute-done | bytes 524320 | tf_op jit(solution)/shard_map/ppermute | solution.py:119
  93.8 0.1 convert_add_fusion.1
  94.0 2.7 %collective-permute-start.7 = (bf16[1,2,256,256]{3,2,1,0:T(8,128)(2,1)S(1)}, bf16[1,2,256,256]{3,2,1,0:T(8,128)(2,1)S(1)}, u32[]{:S(2)}, u32[]{:S(2)}) collective-permute-start(bf16[1,2,256,256]{3,2,1,0:T(8,128)(2,1)S(1)} %slice.61), channel_id=1, source_target_pairs={{0,2},{1,3},{2,0},{3,1},{4,6},{5,7},{6,4},{7,5},{8,10},{9,11},{10,... | collective-permute-start | bytes 786440 | tf_op jit(solution)/shard_map/ppermute | solution.py:119
  96.6 12.2 %collective-permute-done.14 = bf16[2,2,256,256]{3,2,1,0:T(8,128)(2,1)S(1)} collective-permute-done((bf16[2,2,256,256]{3,2,1,0:T(8,128)(2,1)S(1)}, bf16[2,2,256,256]{3,2,1,0:T(8,128)(2,1)S(1)}, u32[]{:S(2)}, u32[]{:S(2)}) %collective-permute-start.14) | collective-permute-done | bytes 524320 | tf_op jit(solution)/shard_map/ppermute | solution.py:119
  108.8 0.1 convert_add_fusion
  109.0 1.8 %collective-permute-start.15 = (bf16[1,2,256,256]{3,2,1,0:T(8,128)(2,1)S(1)}, bf16[1,2,256,256]{3,2,1,0:T(8,128)(2,1)S(1)}, u32[]{:S(2)}, u32[]{:S(2)}) collective-permute-start(bf16[1,2,256,256]{3,2,1,0:T(8,128)(2,1)S(1)} %slice.60), channel_id=1, source_target_pairs={{0,2},{1,3},{2,0},{3,1},{4,6},{5,7},{6,4},{7,5},{8,10},{9,11},{10,... | collective-permute-start | bytes 786440 | tf_op jit(solution)/shard_map/ppermute | solution.py:119
  110.7 0.0 collective-permute-done.7
  110.8 0.1 fusion.1
  110.8 11.3 %collective-permute-done.15 = bf16[1,2,256,256]{3,2,1,0:T(8,128)(2,1)S(1)} collective-permute-done((bf16[1,2,256,256]{3,2,1,0:T(8,128)(2,1)S(1)}, bf16[1,2,256,256]{3,2,1,0:T(8,128)(2,1)S(1)}, u32[]{:S(2)}, u32[]{:S(2)}) %collective-permute-start.15) | collective-permute-done | bytes 262176 | tf_op jit(solution)/shard_map/ppermute | solution.py:119
  122.1 0.1 fusion
  122.2 0.1 maximum_bitcast_fusion
  122.2 0.2 copy.10
  122.4 1.0 copy.11
  (28 shorter events, 0.1 us)
Async XLA Ops:
  1.3 17.9 %copy-start.10 = (bf16[1,512,256]{2,1,0:T(8,128)(2,1)}, bf16[1,512,256]{2,1,0:T(8,128)(2,1)S(1)}, u32[]{:S(2)}) copy-start(bf16[1,512,256]{2,1,0:T(8,128)(2,1)S(1)} %get-tuple-element.15) | copy-start | bytes 786436
  1.3 9.3 %collective-permute-start = (bf16[1,512,256]{2,1,0:T(8,128)(2,1)S(1)}, bf16[1,512,256]{2,1,0:T(8,128)(2,1)S(1)}, u32[]{:S(2)}, u32[]{:S(2)}) collective-permute-start(bf16[1,512,256]{2,1,0:T(8,128)(2,1)S(1)} %get-tuple-element.14), channel_id=1, source_target_pairs={{0,8},{4,12},{8,0},{12,4},{16,24},{20,28},{24,16},{28,20},{1,9},{5... | collective-permute-start | bytes 786440 | tf_op jit(solution)/shard_map/ppermute | solution.py:119
  4.3 9.7 %collective-permute-start.3 = (bf16[1,512,256]{2,1,0:T(8,128)(2,1)S(1)}, bf16[1,512,256]{2,1,0:T(8,128)(2,1)S(1)}, u32[]{:S(2)}, u32[]{:S(2)}) collective-permute-start(bf16[1,512,256]{2,1,0:T(8,128)(2,1)S(1)} %get-tuple-element.13), channel_id=1, source_target_pairs={{0,16},{4,20},{8,24},{12,28},{16,0},{20,4},{24,8},{28,12},{1,17},{... | collective-permute-start | bytes 786440 | tf_op jit(solution)/shard_map/ppermute | solution.py:119
  5.8 13.3 %collective-permute-start.11 = (bf16[1,512,256]{2,1,0:T(8,128)(2,1)S(1)}, bf16[1,512,256]{2,1,0:T(8,128)(2,1)S(1)}, u32[]{:S(2)}, u32[]{:S(2)}) collective-permute-start(bf16[1,512,256]{2,1,0:T(8,128)(2,1)S(1)} %get-tuple-element.15), channel_id=1, source_target_pairs={{0,16},{4,20},{8,24},{12,28},{16,0},{20,4},{24,8},{28,12},{1,17},{... | collective-permute-start | bytes 786440 | tf_op jit(solution)/shard_map/ppermute | solution.py:119
  10.6 19.7 %collective-permute-start.1 = (bf16[2,512,256]{2,1,0:T(8,128)(2,1)S(1)}, bf16[2,512,256]{2,1,0:T(8,128)(2,1)S(1)}, u32[]{:S(2)}, u32[]{:S(2)}) collective-permute-start(bf16[2,512,256]{2,1,0:T(8,128)(2,1)S(1)} %pad_maximum_fusion.4), channel_id=1, source_target_pairs={{0,16},{4,20},{8,24},{12,28},{16,0},{20,4},{24,8},{28,12},{1,17},{... | collective-permute-start | bytes 1572872 | tf_op jit(solution)/shard_map/ppermute | solution.py:119
  12.5 9.2 %collective-permute-start.8 = (bf16[1,512,256]{2,1,0:T(8,128)(2,1)S(1)}, bf16[1,512,256]{2,1,0:T(8,128)(2,1)S(1)}, u32[]{:S(2)}, u32[]{:S(2)}) collective-permute-start(bf16[1,512,256]{2,1,0:T(8,128)(2,1)S(1)} %get-tuple-element.16), channel_id=1, source_target_pairs={{0,8},{4,12},{8,0},{12,4},{16,24},{20,28},{24,16},{28,20},{1,9},{5... | collective-permute-start | bytes 786440 | tf_op jit(solution)/shard_map/ppermute | solution.py:119
  14.0 19.0 %collective-permute-start.4 = (bf16[2,512,256]{2,1,0:T(8,128)(2,1)S(1)}, bf16[2,512,256]{2,1,0:T(8,128)(2,1)}, u32[]{:S(2)}, u32[]{:S(2)}) collective-permute-start(bf16[2,512,256]{2,1,0:T(8,128)(2,1)S(1)} %pad_maximum_fusion.5), channel_id=1, source_target_pairs={{0,8},{4,12},{8,0},{12,4},{16,24},{20,28},{24,16},{28,20},{1,9},{5... | collective-permute-start | bytes 1572872 | tf_op jit(solution)/shard_map/ppermute | solution.py:119
  19.1 0.9 copy-start.12
  20.0 3.0 %copy-start = (bf16[256,1024]{1,0:T(8,128)(2,1)S(1)}, bf16[256,1024]{1,0:T(8,128)(2,1)}, u32[]{:S(2)}) copy-start(bf16[256,1024]{1,0:T(8,128)(2,1)} %k_ref.3) | copy-start | bytes 1572868
  20.0 3.0 %copy-start.2 = (bf16[256,1024]{1,0:T(8,128)(2,1)S(1)}, bf16[256,1024]{1,0:T(8,128)(2,1)}, u32[]{:S(2)}) copy-start(bf16[256,1024]{1,0:T(8,128)(2,1)} %v_ref.3) | copy-start | bytes 1572868
  20.0 24.3 %collective-permute-start.12 = (bf16[2,512,256]{2,1,0:T(8,128)(2,1)}, bf16[2,512,256]{2,1,0:T(8,128)(2,1)}, u32[]{:S(2)}, u32[]{:S(2)}) collective-permute-start(bf16[2,512,256]{2,1,0:T(8,128)(2,1)} %pad_maximum_fusion.7), channel_id=1, source_target_pairs={{0,8},{4,12},{8,0},{12,4},{16,24},{20,28},{24,16},{28,20},{1,9},{5... | collective-permute-start | bytes 1572872 | tf_op jit(solution)/shard_map/ppermute | solution.py:119
  21.7 0.9 copy-start.14
  22.6 22.9 %collective-permute-start.9 = (bf16[2,512,256]{2,1,0:T(8,128)(2,1)}, bf16[2,512,256]{2,1,0:T(8,128)(2,1)}, u32[]{:S(2)}, u32[]{:S(2)}) collective-permute-start(bf16[2,512,256]{2,1,0:T(8,128)(2,1)} %pad_maximum_fusion.6), channel_id=1, source_target_pairs={{0,16},{4,20},{8,24},{12,28},{16,0},{20,4},{24,8},{28,12},{1,17},{... | collective-permute-start | bytes 1572872 | tf_op jit(solution)/shard_map/ppermute | solution.py:119
  24.0 29.1 %all-to-all-start = ((bf16[8,128,256]{2,1,0:T(8,128)(2,1)}), bf16[8,128,256]{2,1,0:T(8,128)(2,1)}, u32[]{:S(2)}, u32[]{:S(2)}) async-start(bf16[8,128,256]{2,1,0:T(8,128)(2,1)} %bitcast.5), calls=%async_computation | async-start | bytes 1048576 | tf_op jit(solution)/shard_map/all_to_all | solution.py:168
  30.5 13.8 %copy-start.11 = (bf16[1,512,256]{2,1,0:T(8,128)(2,1)S(1)}, bf16[1,512,256]{2,1,0:T(8,128)(2,1)}, u32[]{:S(2)}) copy-start(bf16[1,512,256]{2,1,0:T(8,128)(2,1)} %copy-done.10) | copy-start | bytes 786436
  30.5 13.8 %copy-start.13 = (bf16[1,512,256]{2,1,0:T(8,128)(2,1)S(1)}, bf16[1,512,256]{2,1,0:T(8,128)(2,1)}, u32[]{:S(2)}) copy-start(bf16[1,512,256]{2,1,0:T(8,128)(2,1)} %copy-done.12) | copy-start | bytes 786436
  30.5 43.4 %collective-permute-start.2 = (bf16[4,512,256]{2,1,0:T(8,128)(2,1)S(1)}, bf16[4,512,256]{2,1,0:T(8,128)(2,1)}, u32[]{:S(2)}, u32[]{:S(2)}) collective-permute-start(bf16[4,512,256]{2,1,0:T(8,128)(2,1)S(1)} %pad_maximum_fusion.refs_0_), channel_id=1, source_target_pairs={{0,4},{4,0},{8,12},{12,8},{16,20},{20,16},{24,28},{28,24},{1,5},{5... | collective-permute-start | bytes 3145736 | tf_op jit(solution)/shard_map/ppermute | solution.py:119
  34.2 11.3 %copy-start.15 = (bf16[1,512,256]{2,1,0:T(8,128)(2,1)S(1)}, bf16[1,512,256]{2,1,0:T(8,128)(2,1)}, u32[]{:S(2)}) copy-start(bf16[1,512,256]{2,1,0:T(8,128)(2,1)} %copy-done.14) | copy-start | bytes 786436
  34.2 39.7 %collective-permute-start.5 = (bf16[4,512,256]{2,1,0:T(8,128)(2,1)S(1)}, bf16[4,512,256]{2,1,0:T(8,128)(2,1)}, u32[]{:S(2)}, u32[]{:S(2)}) collective-permute-start(bf16[4,512,256]{2,1,0:T(8,128)(2,1)S(1)} %pad_maximum_fusion.1.refs_2_), channel_id=1, source_target_pairs={{0,4},{4,0},{8,12},{12,8},{16,20},{20,16},{24,28},{28,24},{1,5},{5... | collective-permute-start | bytes 3145736 | tf_op jit(solution)/shard_map/ppermute | solution.py:119
  45.4 35.1 %collective-permute-start.13 = (bf16[4,512,256]{2,1,0:T(8,128)(2,1)S(1)}, bf16[4,512,256]{2,1,0:T(8,128)(2,1)}, u32[]{:S(2)}, u32[]{:S(2)}) collective-permute-start(bf16[4,512,256]{2,1,0:T(8,128)(2,1)S(1)} %pad_maximum_fusion.3.refs_2_), channel_id=1, source_target_pairs={{0,4},{4,0},{8,12},{12,8},{16,20},{20,16},{24,28},{28,24},{1,5},{5... | collective-permute-start | bytes 3145736 | tf_op jit(solution)/shard_map/ppermute | solution.py:119
  45.5 2.7 %copy-start.5 = (f32[64,64]{1,0:T(8,128)S(1)}, f32[64,64]{1,0:T(8,128)}, u32[]{:S(2)}) copy-start(f32[64,64]{1,0:T(8,128)} %fout_ref.1) | copy-start | bytes 49156
  45.6 2.7 %copy-start.9 = (f32[64]{0:T(128)S(1)}, f32[64]{0:T(128)}, u32[]{:S(2)}) copy-start(f32[64]{0:T(128)} %param.15) | copy-start | bytes 772
  47.7 0.7 copy-start.6
  47.7 32.9 %collective-permute-start.10 = (bf16[4,512,256]{2,1,0:T(8,128)(2,1)}, bf16[4,512,256]{2,1,0:T(8,128)(2,1)}, u32[]{:S(2)}, u32[]{:S(2)}) collective-permute-start(bf16[4,512,256]{2,1,0:T(8,128)(2,1)} %pad_maximum_fusion.2.refs_0_), channel_id=1, source_target_pairs={{0,4},{4,0},{8,12},{12,8},{16,20},{20,16},{24,28},{28,24},{1,5},{5... | collective-permute-start | bytes 3145736 | tf_op jit(solution)/shard_map/ppermute | solution.py:119
  48.2 0.7 copy-start.8
  53.1 20.4 %copy-start.4 = (bf16[256,1024]{1,0:T(8,128)(2,1)S(1)}, bf16[256,1024]{1,0:T(8,128)(2,1)}, u32[]{:S(2)}) copy-start(bf16[256,1024]{1,0:T(8,128)(2,1)} %q_ref.1) | copy-start | bytes 1572868
  53.1 20.4 %copy-start.7 = (f32[1024]{0:T(1024)S(1)}, f32[1024]{0:T(1024)}, u32[]{:S(2)}) copy-start(f32[1024]{0:T(1024)} %param.16) | copy-start | bytes 12292
  61.0 12.5 %copy-start.1 = (bf16[256,1024]{1,0:T(8,128)(2,1)S(1)}, bf16[256,1024]{1,0:T(8,128)(2,1)}, u32[]{:S(2)}) copy-start(bf16[256,1024]{1,0:T(8,128)(2,1)} %k_ref.3) | copy-start | bytes 1572868
  61.0 12.5 %copy-start.3 = (bf16[256,1024]{1,0:T(8,128)(2,1)S(1)}, bf16[256,1024]{1,0:T(8,128)(2,1)}, u32[]{:S(2)}) copy-start(bf16[256,1024]{1,0:T(8,128)(2,1)} %v_ref.3) | copy-start | bytes 1572868
  78.9 14.9 %collective-permute-start.6 = (bf16[2,2,256,256]{3,2,1,0:T(8,128)(2,1)S(1)}, bf16[2,2,256,256]{3,2,1,0:T(8,128)(2,1)S(1)}, u32[]{:S(2)}, u32[]{:S(2)}) collective-permute-start(bf16[2,2,256,256]{3,2,1,0:T(8,128)(2,1)S(1)} %get-tuple-element.10), channel_id=1, source_target_pairs={{0,1},{1,0},{2,3},{3,2},{4,5},{5,4},{6,7},{7,6},{8,9},{9,8},{10,11... | collective-permute-start | bytes 1572872 | tf_op jit(solution)/shard_map/ppermute | solution.py:119
  85.9 22.9 %collective-permute-start.14 = (bf16[2,2,256,256]{3,2,1,0:T(8,128)(2,1)S(1)}, bf16[2,2,256,256]{3,2,1,0:T(8,128)(2,1)S(1)}, u32[]{:S(2)}, u32[]{:S(2)}) collective-permute-start(bf16[2,2,256,256]{3,2,1,0:T(8,128)(2,1)S(1)} %get-tuple-element.12), channel_id=1, source_target_pairs={{0,1},{1,0},{2,3},{3,2},{4,5},{5,4},{6,7},{7,6},{8,9},{9,8},{10,11... | collective-permute-start | bytes 1572872 | tf_op jit(solution)/shard_map/ppermute | solution.py:119
  94.0 16.8 %collective-permute-start.7 = (bf16[1,2,256,256]{3,2,1,0:T(8,128)(2,1)S(1)}, bf16[1,2,256,256]{3,2,1,0:T(8,128)(2,1)S(1)}, u32[]{:S(2)}, u32[]{:S(2)}) collective-permute-start(bf16[1,2,256,256]{3,2,1,0:T(8,128)(2,1)S(1)} %slice.61), channel_id=1, source_target_pairs={{0,2},{1,3},{2,0},{3,1},{4,6},{5,7},{6,4},{7,5},{8,10},{9,11},{10,... | collective-permute-start | bytes 786440 | tf_op jit(solution)/shard_map/ppermute | solution.py:119
  109.0 13.1 %collective-permute-start.15 = (bf16[1,2,256,256]{3,2,1,0:T(8,128)(2,1)S(1)}, bf16[1,2,256,256]{3,2,1,0:T(8,128)(2,1)S(1)}, u32[]{:S(2)}, u32[]{:S(2)}) collective-permute-start(bf16[1,2,256,256]{3,2,1,0:T(8,128)(2,1)S(1)} %slice.60), channel_id=1, source_target_pairs={{0,2},{1,3},{2,0},{3,1},{4,6},{5,7},{6,4},{7,5},{8,10},{9,11},{10,... | collective-permute-start | bytes 786440 | tf_op jit(solution)/shard_map/ppermute | solution.py:119

commit v2 on v1

v2 whole, which is shorter than its diff:
```python
import functools
import math

import jax
import jax.numpy as jnp
from jax import lax
from jax.experimental import pallas as pl
from jax.experimental.pallas import tpu as pltpu
from jax.sharding import PartitionSpec as P

BF = jnp.bfloat16
F32 = jnp.float32
LANE = 128
SUB = 16
CHUNK = 256
FULL = pltpu.CompilerParams(vmem_limit_bytes=64 * 1024 * 1024)
PARAMS = pltpu.CompilerParams(vmem_limit_bytes=48 * 1024 * 1024)
SMEM = pl.BlockSpec(memory_space=pltpu.SMEM)
VMEM = pl.BlockSpec(memory_space=pltpu.VMEM)
ANY = pl.BlockSpec(memory_space=pl.ANY)
HBM = pl.BlockSpec(memory_space=pltpu.HBM)
DMA = pltpu.SemaphoreType.DMA


def sine(x):
    n = jnp.round(x * (1.0 / math.pi))
    r = x - n * 3.140625
    r = r - n * 9.67502593994140625e-4
    r = r - n * 1.509957990978376432e-7
    s = r * r
    p = jnp.float32(2.6083159809786593541503e-06)
    p = p * s - 1.981069071916863322258e-04
    p = p * s + 8.33307858556509017944336e-03
    p = p * s - 1.66666597127914428710938e-01
    y = r + r * (s * p)
    return jnp.where((n.astype(jnp.int32) & 1) == 1, -y, y)


def first_kernel(k_hbm, v_hbm, u_hbm, k_ref, v_ref, u_ref, sems, done):
    steps = sems.shape[0]
    part = k_hbm.shape[1] // steps
    spans = [slice(part * i, part * (i + 1)) for i in range(steps)]
    loads = []
    for i, at in enumerate(spans):
        loads.append(pltpu.make_async_copy(k_hbm.at[:, at], k_ref.at[:, at], sems.at[i, 0]))
        loads.append(pltpu.make_async_copy(v_hbm.at[:, at], v_ref.at[:, at], sems.at[i, 1]))
    for load in loads:
        load.start()
    stores = []
    for i, at in enumerate(spans):
        loads[2 * i].wait()
        loads[2 * i + 1].wait()
        prod = k_ref[:, at].astype(F32) * v_ref[:, at].astype(F32)
        u_ref[at, :] = prod.T.astype(BF)
        stores.append(pltpu.make_async_copy(u_ref.at[at], u_hbm.at[at], done.at[i]))
        stores[i].start()
    for store in stores:
        store.wait()


def taps_kernel(
    seq, me_ref, fin_hbm, bias_hbm, fout_hbm, decay_hbm, w_hbm, u_hbm, o_ref, *rest
):
    cuts, held, sems, cut_sems = rest[:-6], rest[-6:-2], rest[-2], rest[-1]
    moves, at = [], 0
    for n, cut in enumerate(cuts):
        half, size = cut.shape[1:]
        for m in range(2):
            source = w_hbm.at[pl.ds(half * m, half), pl.ds(at, size)]
            moves.append(pltpu.make_async_copy(source, cut.at[m], cut_sems.at[n, m]))
        at += size
    loads = [
        pltpu.make_async_copy(source, target, sems.at[i])
        for i, (source, target) in enumerate(zip((fin_hbm, bias_hbm, fout_hbm, decay_hbm), held))
    ]
    for load in loads + moves:
        load.start()
    for load in loads:
        load.wait()
    fin_ref, bias_ref, fout_ref, decay_ref = held
    bands = (fin_ref.shape[0] - 1) // 2
    groups = o_ref.shape[0]
    all_groups = fout_ref.shape[1]
    contract = functools.partial(
        lax.dot_general, precision=lax.Precision.HIGHEST, preferred_element_type=F32
    )
    first = (((0,), (0,)), ((), ()))
    harmonic = lax.broadcasted_iota(jnp.int32, (bands, seq), 0) + 1
    lag = lax.broadcasted_iota(jnp.int32, (bands, seq), 1)
    phase = lax.rem(harmonic * lag, seq).astype(F32) * (2.0 * math.pi / seq)
    time = lax.broadcasted_iota(jnp.int32, (1, seq), 1).astype(F32)
    pre = contract(fin_ref[1 : 1 + bands, :], sine(phase + math.pi / 2), first)
    pre += contract(fin_ref[1 + bands : 1 + 2 * bands, :], sine(phase), first)
    pre += contract(fin_ref[0:1, :], time / seq, first)
    pre += contract(bias_ref[...], jnp.ones((1, seq), F32), first)
    hidden = sine(pre)
    row = lax.broadcasted_iota(jnp.int32, (groups, all_groups), 0)
    col = lax.broadcasted_iota(jnp.int32, (groups, all_groups), 1)
    pick = (col == me_ref[0] * groups + row).astype(F32)
    fout = contract(pick, fout_ref[...], (((1,), (1,)), ((), ())))
    decay = jnp.sum(pick * decay_ref[...], axis=1, keepdims=True)
    raw = contract(fout, hidden, (((1,), (0,)), ((), ())))
    o_ref[:, :LANE] = jnp.zeros((groups, LANE), F32)
    o_ref[:, LANE:] = (raw * jnp.exp(-decay * time)).astype(BF).astype(F32)
    for move in moves:
        move.wait()


def conv_kernel(seq, width, taps_ref, u_hbm, o_hbm, rev, toep, out_ref, sems, done):
    blocks = seq // LANE
    per = u_hbm.shape[2] // LANE
    groups = taps_ref.shape[0]
    loads = []
    for a in range(blocks):
        source = u_hbm.at[a // per, :, pl.ds(LANE * (a % per), LANE)]
        target = rev.at[:, pl.ds(LANE * (blocks - 1 - a), LANE)]
        loads.append(pltpu.make_async_copy(source, target, sems.at[a]))
        loads[a].start()
    rev[:, seq:] = jnp.zeros((rev.shape[0], rev.shape[1] - seq), BF)
    stores = []
    for g in range(groups):
        line = jnp.broadcast_to(taps_ref[g : g + 1, :], (SUB, LANE + seq))
        slab = pltpu.roll(line, 0, 1, stride=1, stride_axis=0)
        for k in range(LANE // SUB):
            part = (slab if k == 0 else pltpu.roll(slab, SUB * k, 1)).astype(BF)
            for d in range(blocks):
                toep[g % 2, LANE * d + SUB * k : LANE * d + SUB * (k + 1), :] = part[
                    :, LANE * (d + 1) : LANE * (d + 2)
                ]
        if g == 0:
            for load in loads:
                load.wait()
        mine = slice(width * g, width * (g + 1))
        starts = [LANE * (blocks - 1 - b) for b in range(blocks)]
        lhs = jnp.concatenate([rev[mine, at : at + seq] for at in starts], 0)
        out = jnp.dot(lhs, toep[g % 2], preferred_element_type=F32).astype(BF)
        for b in range(blocks):
            out_ref[b // per, mine, LANE * (b % per) : LANE * (b % per + 1)] = out[
                width * b : width * (b + 1), :
            ]
        stores.append(
            pltpu.make_async_copy(out_ref.at[:, mine], o_hbm.at[:, mine], done.at[g])
        )
        stores[g].start()
    for store in stores:
        store.wait()


def gate_kernel(q_hbm, k_hbm, v_hbm, skip_hbm, conv_hbm, o_ref, q_ref, k_ref, v_ref, skip_ref, conv_ref, sems):
    steps = sems.shape[0]
    part = q_hbm.shape[1] // steps
    spans = [slice(part * i, part * (i + 1)) for i in range(steps)]
    pairs = ((q_hbm, q_ref), (k_hbm, k_ref), (v_hbm, v_ref), (skip_hbm, skip_ref))
    loads = []
    for i, at in enumerate(spans):
        step = [pltpu.make_async_copy(conv_hbm.at[at], conv_ref.at[at], sems.at[i, 4])]
        for n, (source, target) in enumerate(pairs):
            step.append(pltpu.make_async_copy(source.at[:, at], target.at[:, at], sems.at[i, n]))
        for load in step:
            load.start()
        loads.append(step)
    for i, at in enumerate(spans):
        for load in loads[i]:
            load.wait()
        u = (k_ref[:, at].astype(F32) * v_ref[:, at].astype(F32)).astype(BF).astype(F32)
        conv = conv_ref[at, :].astype(F32).T
        gated = q_ref[:, at].astype(F32) * (conv + skip_ref[:, at] * u)
        o_ref[:, at] = gated.astype(BF)


def block_kernel(r, place_ref, x_ref, y_ref, own_ref, by_x_ref, by_y_ref, far_0_ref, far_1_ref, o_ref, held, sems):
    half = held.shape[0] // 2
    rows = x_ref.shape[0]
    chip = jnp.bitwise_xor(jnp.bitwise_xor(place_ref[1], r), place_ref[0] // 2)
    sources = [(own_ref.at[0], own_ref.at[1]), (by_x_ref.at[0], by_x_ref.at[1])]
    sources += [(by_y_ref.at[0], by_y_ref.at[1]), (far_0_ref.at[0], far_1_ref.at[0])]
    for choice, parts in enumerate(sources):

        @pl.when(chip == choice)
        def _():
            for n, part in enumerate(parts):
                pltpu.make_async_copy(
                    part, held.at[pl.ds(half * n, half)], sems.at[n]
                ).start()

    for n in range(2):
        pltpu.make_async_copy(
            own_ref.at[n], held.at[pl.ds(half * n, half)], sems.at[n]
        ).wait()
    o_ref[:rows] = jnp.dot(x_ref[...], held[...], preferred_element_type=F32).astype(BF)
    o_ref[rows:] = jnp.dot(y_ref[...], held[...], preferred_element_type=F32).astype(BF)


def last_kernel(chunks, place_ref, *refs):
    o_ref = refs[-1]
    core = place_ref[0] % 2
    at = 0
    for n, size in enumerate(chunks):
        for half, ref in ((core, refs[2 * n]), (1 - core, refs[2 * n + 1])):
            to = pl.multiple_of(half * (o_ref.shape[1] // 2) + at, LANE)
            o_ref[:, pl.ds(to, size)] = ref[...]
        at += size


def after_kernel(count, *refs):
    pass


def after(values, *others):
    values = list(values)
    count = len(values)
    return pl.pallas_call(
        functools.partial(after_kernel, count),
        out_shape=[jax.ShapeDtypeStruct(v.shape, v.dtype) for v in values],
        in_specs=[ANY] * (count + len(others)),
        out_specs=[ANY] * count,
        input_output_aliases={i: i for i in range(count)},
        compiler_params=PARAMS,
    )(*values, *others)


def swap(value, axis, bit):
    count = lax.axis_size(axis)
    return lax.ppermute(value, axis, [(i, i ^ bit) for i in range(count)])


def project_pairs(place, gated, cuts, conv_all):
    rows = gated.shape[0]
    call = functools.partial(pl.pallas_call, compiler_params=PARAMS)
    shape = jax.ShapeDtypeStruct
    other = swap(gated, "ctx", 1)
    finals = []
    previous = (conv_all,)
    for number, cut in enumerate(cuts):
        depth, n = 2 * cut.shape[1], cut.shape[2]
        if number:
            (cut,) = after([cut], *gate)
        by_x, by_y = swap(cut, "ctx", 2), swap(cut, "ctx", 4)
        by_x, by_y = after([by_x, by_y], *previous)
        far_1 = swap(by_x[1:], "ctx", 4)
        far_0 = swap(by_y[:1], "ctx", 2)
        gate = (far_0, far_1)
        blocks = {}
        for r in (3, 1, 2, 0):
            blocks[r] = call(
                functools.partial(block_kernel, r),
                out_shape=shape((2 * rows, n), BF),
                in_specs=[SMEM, VMEM, VMEM] + [ANY] * 5,
                scratch_shapes=[
                    pltpu.VMEM((depth, n), BF),
                    pltpu.SemaphoreType.DMA((2,)),
                ],
            )(place, gated, other, cut, by_x, by_y, far_0, far_1)
        got_3 = swap(blocks[3], "ch", 1)
        got_1 = swap(blocks[1], "ch", 1)
        previous = (got_3, got_1)
        two = (blocks[2].astype(F32) + got_3.astype(F32)).astype(BF)
        got_2 = swap(two, "ch", 2)
        total = blocks[0].astype(F32) + got_1.astype(F32) + got_2.astype(F32)
        mine, theirs = total[:rows].astype(BF), total[rows:].astype(BF)
        finals += [mine, swap(theirs, "ctx", 1)]
    return call(
        functools.partial(last_kernel, [c.shape[2] for c in cuts]),
        out_shape=shape((rows, 2 * sum(c.shape[2] for c in cuts)), BF),
        in_specs=[SMEM] + [VMEM] * len(finals),
    )(place, *finals)


def local(
    query_proj,
    key_proj,
    value_proj,
    filter_in,
    filter_bias,
    filter_out,
    decay_rates,
    skip_gain,
    out_weight,
):
    ctx_count = lax.axis_size("ctx")
    ch_count = lax.axis_size("ch")
    rows, channels = query_proj.shape
    seq = rows * ctx_count
    width = channels // filter_out.shape[1]
    own = channels // ctx_count
    depth, columns = out_weight.shape
    pairs = ctx_count == 8 and ch_count == 4
    me = lax.axis_index("ctx")
    z = lax.axis_index("ch")
    place = jnp.stack([me, z]).astype(jnp.int32)
    call = functools.partial(pl.pallas_call, compiler_params=PARAMS)
    shape = jax.ShapeDtypeStruct

    chunks = [CHUNK] * (columns // CHUNK) if pairs else []
    steps = 4
    groups = own // width
    u_t = pl.pallas_call(
        first_kernel,
        compiler_params=FULL,
        out_shape=shape((channels, rows), BF),
        in_specs=[HBM, HBM],
        out_specs=HBM,
        scratch_shapes=[
            pltpu.VMEM((rows, channels), BF),
            pltpu.VMEM((rows, channels), BF),
            pltpu.VMEM((channels, rows), BF),
            DMA((steps, 2)),
            DMA((steps,)),
        ],
    )(key_proj, value_proj)
    u_all = lax.all_to_all(u_t.reshape(ctx_count, own, rows), "ctx", 0, 0)
    small = (filter_in, filter_bias[None], filter_out, decay_rates[None])
    taps, *cuts = call(
        functools.partial(taps_kernel, seq),
        out_shape=[shape((groups, LANE + seq), F32)]
        + [shape((2, depth // 2, n), BF) for n in chunks],
        in_specs=[SMEM] + [HBM] * 6,
        out_specs=[VMEM] + [HBM] * len(chunks),
        scratch_shapes=[pltpu.VMEM(a.shape, F32) for a in small]
        + [DMA((4,)), DMA((max(1, len(chunks)), 2))],
    )(place, *small, out_weight, u_t)
    conv_all = call(
        functools.partial(conv_kernel, seq, width),
        out_shape=shape(u_all.shape, BF),
        in_specs=[VMEM, HBM],
        out_specs=HBM,
        scratch_shapes=[
            pltpu.VMEM((own, 2 * seq), BF),
            pltpu.VMEM((2, seq, LANE), BF),
            pltpu.VMEM(u_all.shape, BF),
            DMA((seq // LANE,)),
            DMA((groups,)),
        ],
    )(taps, u_all)
    conv_t = lax.all_to_all(conv_all, "ctx", 0, 0).reshape(channels, rows)
    gated = call(
        gate_kernel,
        out_shape=shape((rows, channels), BF),
        in_specs=[HBM] * 5,
        out_specs=VMEM,
        scratch_shapes=[pltpu.VMEM((rows, channels), BF)] * 3
        + [
            pltpu.VMEM((1, channels), F32),
            pltpu.VMEM((channels, rows), BF),
            DMA((steps, 5)),
        ],
    )(query_proj, key_proj, value_proj, skip_gain[None], conv_t)
    if pairs:
        return project_pairs(place, gated, cuts, conv_all)
    everything = lax.all_gather(out_weight, "ctx", axis=1, tiled=True)
    sums = jnp.dot(gated, everything, preferred_element_type=F32).astype(BF)
    return lax.psum_scatter(sums, "ch", scatter_dimension=1, tiled=True)


def solution(mesh):
    placed = (
        P("ctx", "ch"),
        P("ctx", "ch"),
        P("ctx", "ch"),
        P(),
        P(),
        P(None, "ch"),
        P("ch"),
        P("ch"),
        P("ch", "ctx"),
    )
    return jax.shard_map(
        local, mesh=mesh, in_specs=placed, out_specs=P("ctx", "ch"), check_vma=False
    )
```

time: 124 us -> 96.2 us (0.78)
  waiting for transfers between devices: 56.1 us -> 38.6 us
  blocking collectives: 12.4 us -> 0 us
  starting transfers between devices: 20.8 us -> 29.5 us
  other arithmetic: 6.86 us -> 0.43 us
  Pallas kernels: 23.8 us -> 22.1 us
  local copies, waits for them, and re-layouts: 3.24 us -> 4.79 us
    ppermute x16 -> x17, waiting for transfers between devices: 56.1 us -> 30.9 us  [swap(): return lax.ppermute(value, axis, [(i, i ^ bit) for i in range(count)])]
    all_to_all x1 -> x0, blocking collectives: 12.4 us -> none  [local(): conv_t = lax.all_to_all(conv_all, 'ctx', 0, 0).reshape(channels, rows)]
    concatenate x8 -> x0, other arithmetic: 6.38 us -> none  [gather_half(): held = jnp.concatenate([held, swap(held, 'ctx', bit)], 0)]
    all_to_all x0 -> x1, waiting for transfers between devices: none -> 6.05 us  [local(): conv_t = lax.all_to_all(conv_all, 'ctx', 0, 0).reshape(channels, rows)]
    all_to_all x0 -> x1, starting transfers between devices: none -> 4.16 us  [local(): conv_t = lax.all_to_all(conv_all, 'ctx', 0, 0).reshape(channels, rows)]
    ppermute x16 -> x17, starting transfers between devices: 16.6 us -> 20.1 us  [swap(): return lax.ppermute(value, axis, [(i, i ^ bit) for i in range(count)])]
    unnamed x32 -> x20, local copies, waits for them, and re-layouts: 0.72 us -> 3.98 us
    pallas_call x6 -> x16, Pallas kernels: 23.8 us -> 22.1 us  [the longest x8 8.53 us: project_pairs(): call(functools.partial(block_kernel, r), out_shape=shape((2 * rows, n), B...]
  transfers between devices with their start and end apart: 17 -> 19, of which waited for: 9 -> 15; matrix products, arithmetic and copies ran while one was open for 6% -> 1% of each run, Pallas kernels for 19% -> 18%
where the time goes in v2:
time: 96.2 us; the launch traced here: 95.6 us
  waiting for transfers between devices  38.6 us (40%)
  starting transfers between devices  29.5 us (31%)
  Pallas kernels  22.1 us (23%)
  local copies, waits for them, and re-layouts  4.79 us (5%)
    ppermute x17, waiting for transfers between devices, swap(): return lax.ppermute(value, axis, [(i, i ^ bit) for i in range(count)])  30.9 us
    ppermute x17, starting transfers between devices, swap(): return lax.ppermute(value, axis, [(i, i ^ bit) for i in range(count)])  20.1 us
    pallas_call x8, Pallas kernels, project_pairs(): call(functools.partial(block_kernel, r), out_shape=shape((2 * rows, n), B...  8.53 us
    all_to_all x1, waiting for transfers between devices, local(): conv_t = lax.all_to_all(conv_all, 'ctx', 0, 0).reshape(channels, rows)  6.05 us
    pallas_call x1, Pallas kernels, local(): call(functools.partial(conv_kernel, seq, width), out_shape=shape(u_all.sh...  5.43 us
    all_to_all x1, starting transfers between devices, local(): u_all = lax.all_to_all(u_t.reshape(ctx_count, own, rows), 'ctx', 0, 0)  5.31 us
    all_to_all x1, starting transfers between devices, local(): conv_t = lax.all_to_all(conv_all, 'ctx', 0, 0).reshape(channels, rows)  4.16 us
    unnamed x20, local copies, waits for them, and re-layouts  3.98 us
  transfers between devices with their start and end apart: 19, of which 15 were waited for; matrix products, arithmetic and copies ran while one was open for 1% of the time, Pallas kernels for 18%

profile of v2, /device:TPU:0, one launch (start us, length us, event | category | flops | bytes accessed | tf_op | source)
XLA Modules:
  0.0 95.6 jit_solution(12869428224287560190)
XLA Ops:
  0.0 2.2 %shard_map.91.u_hbm = bf16[1024,256]{1,0:T(8,128)(2,1)} custom-call(bf16[256,1024]{1,0:T(8,128)(2,1)} %k_hbm.3, bf16[256,1024]{1,0:T(8,128)(2,1)} %v_hbm.3), custom_call_target="tpu_custom_call" | custom-call | tf_op jit(solution)/shard_map/pallas_call | solution.py:297
  2.2 0.0 copy-start
  2.2 0.0 copy-start.5
  2.2 0.0 copy-start.9
  2.2 5.3 %all-to-all-start = ((bf16[8,128,256]{2,1,0:T(8,128)(2,1)}), bf16[8,128,256]{2,1,0:T(8,128)(2,1)S(1)}, u32[]{:S(2)}, u32[]{:S(2)}) async-start(bf16[8,128,256]{2,1,0:T(8,128)(2,1)} %bitcast.7), calls=%async_computation | async-start | bytes 1048576 | tf_op jit(solution)/shard_map/all_to_all | solution.py:311
  7.6 0.1 pad_add_fusion.me_ref.place_ref
  7.6 0.6 copy-done.6
  8.3 0.0 copy-done.8
  8.3 1.2 %copy-done.3 = bf16[1024,512]{1,0:T(8,128)(2,1)S(1)} copy-done((bf16[1024,512]{1,0:T(8,128)(2,1)S(1)}, bf16[1024,512]{1,0:T(8,128)(2,1)}, u32[]{:S(2)}) %copy-start.3) | copy-done | bytes 1048600
  9.5 3.0 %shard_map.92 = (f32[8,2176]{1,0:T(8,128)S(1)}, bf16[2,512,256]{2,1,0:T(8,128)(2,1)S(1)}, bf16[2,512,256]{2,1,0:T(8,128)(2,1)S(1)}) custom-call(s32[2]{0:T(128)S(1)} %pad_add_fusion.me_ref.place_ref, f32[33,64]{1,0:T(8,128)S(1)} %copy-done.6, f32[1,64]{1,0:T(1,128)S(1)} %bitcast.9, f32[64,64]{1,0:T(8,128)S(1)} %copy-done.5, f32[1,64]{1,0:T(1,128)S(1)} %bitcast.10, ...), custom_call_target="tpu_custom_call" | custom-call | tf_op jit(solution)/shard_map/pallas_call | solution.py:313
  12.5 2.1 %collective-permute-start.2 = (bf16[2,512,256]{2,1,0:T(8,128)(2,1)S(1)}, bf16[2,512,256]{2,1,0:T(8,128)(2,1)S(1)}, u32[]{:S(2)}, u32[]{:S(2)}) collective-permute-start(bf16[2,512,256]{2,1,0:T(8,128)(2,1)S(1)} %get-tuple-element.13.own_ref), channel_id=1, source_target_pairs={{0,16},{4,20},{8,24},{12,28},{16,0},{20,4},{24,8},{28,12},{1,17},{... | collective-permute-start | bytes 1572872 | tf_op jit(solution)/shard_map/ppermute | solution.py:224
  14.6 1.5 %collective-permute-start.1 = (bf16[2,512,256]{2,1,0:T(8,128)(2,1)S(1)}, bf16[2,512,256]{2,1,0:T(8,128)(2,1)S(1)}, u32[]{:S(2)}, u32[]{:S(2)}) collective-permute-start(bf16[2,512,256]{2,1,0:T(8,128)(2,1)S(1)} %get-tuple-element.13.own_ref), channel_id=1, source_target_pairs={{0,8},{4,12},{8,0},{12,4},{16,24},{20,28},{24,16},{28,20},{1,9},{5... | collective-permute-start | bytes 1572872 | tf_op jit(solution)/shard_map/ppermute | solution.py:224
  16.0 1.7 %all-to-all-done.u_hbm = bf16[8,128,256]{2,1,0:T(8,128)(2,1)S(1)} async-done(((bf16[8,128,256]{2,1,0:T(8,128)(2,1)}), bf16[8,128,256]{2,1,0:T(8,128)(2,1)S(1)}, u32[]{:S(2)}, u32[]{:S(2)}) %all-to-all-start) | async-done | bytes 524320 | tf_op jit(solution)/shard_map/all_to_all | solution.py:311
  17.7 5.4 %shard_map.93.refs_2_ = bf16[8,128,256]{2,1,0:T(8,128)(2,1)} custom-call(f32[8,2176]{1,0:T(8,128)S(1)} %get-tuple-element.12.taps_ref, bf16[8,128,256]{2,1,0:T(8,128)(2,1)S(1)} %all-to-all-done.u_hbm), custom_call_target="tpu_custom_call" | custom-call | tf_op jit(solution)/shard_map/pallas_call | solution.py:322
  23.1 4.2 %all-to-all-start.1 = ((bf16[8,128,256]{2,1,0:T(8,128)(2,1)}), bf16[8,128,256]{2,1,0:T(8,128)(2,1)}, u32[]{:S(2)}, u32[]{:S(2)}) async-start(bf16[8,128,256]{2,1,0:T(8,128)(2,1)} %shard_map.93.refs_2_), calls=%async_computation.1 | async-start | bytes 1048576 | tf_op jit(solution)/shard_map/all_to_all | solution.py:335
  27.3 0.9 collective-permute-done.2.refs_1_
  28.2 0.1 collective-permute-done.1.refs_0_
  28.3 0.0 copy-start.7
  28.3 0.7 slice.28
  29.0 1.5 %collective-permute-start.3 = (bf16[1,512,256]{2,1,0:T(8,128)(2,1)}, bf16[1,512,256]{2,1,0:T(8,128)(2,1)S(1)}, u32[]{:S(2)}, u32[]{:S(2)}) collective-permute-start(bf16[1,512,256]{2,1,0:T(8,128)(2,1)} %slice.28), channel_id=1, source_target_pairs={{0,8},{4,12},{8,0},{12,4},{16,24},{20,28},{24,16},{28,20},{1,9},{5... | collective-permute-start | bytes 786440 | tf_op jit(solution)/shard_map/ppermute | solution.py:224
  30.5 1.0 %collective-permute-start.4 = (bf16[1,512,256]{2,1,0:T(8,128)(2,1)S(1)}, bf16[1,512,256]{2,1,0:T(8,128)(2,1)S(1)}, u32[]{:S(2)}, u32[]{:S(2)}) collective-permute-start(bf16[1,512,256]{2,1,0:T(8,128)(2,1)S(1)} %slice.29), channel_id=1, source_target_pairs={{0,16},{4,20},{8,24},{12,28},{16,0},{20,4},{24,8},{28,12},{1,17},{... | collective-permute-start | bytes 786440 | tf_op jit(solution)/shard_map/ppermute | solution.py:224
  31.5 6.0 %all-to-all-done.1 = bf16[8,128,256]{2,1,0:T(8,128)(2,1)} async-done(((bf16[8,128,256]{2,1,0:T(8,128)(2,1)}), bf16[8,128,256]{2,1,0:T(8,128)(2,1)}, u32[]{:S(2)}, u32[]{:S(2)}) %all-to-all-start.1) | async-done | bytes 524320 | tf_op jit(solution)/shard_map/all_to_all | solution.py:335
  37.5 1.0 %copy-done.2 = bf16[256,1024]{1,0:T(8,128)(2,1)S(1)} copy-done((bf16[256,1024]{1,0:T(8,128)(2,1)S(1)}, bf16[256,1024]{1,0:T(8,128)(2,1)}, u32[]{:S(2)}) %copy-start.2) | copy-done | bytes 524312
  38.6 1.0 %copy-done.4 = bf16[256,1024]{1,0:T(8,128)(2,1)S(1)} copy-done((bf16[256,1024]{1,0:T(8,128)(2,1)S(1)}, bf16[256,1024]{1,0:T(8,128)(2,1)}, u32[]{:S(2)}) %copy-start.4) | copy-done | bytes 524312
  39.6 1.5 %shard_map.94.x_ref = bf16[256,1024]{1,0:T(8,128)(2,1)S(1)} custom-call(bf16[256,1024]{1,0:T(8,128)(2,1)S(1)} %copy-done.4, bf16[256,1024]{1,0:T(8,128)(2,1)S(1)} %copy-done.1, bf16[256,1024]{1,0:T(8,128)(2,1)S(1)} %copy-done.2, f32[1,1024]{1,0:T(1,128)S(1)} %bitcast.8, bf16[1024,256]{1,0:T(8,128)(2,1)} %bitcast.6.conv_hbm), custom_call_target="tpu_custom_call" | custom-call | tf_op jit(solution)/shard_map/pallas_call | solution.py:336
  41.2 0.1 collective-permute-start
  41.2 0.4 collective-permute-done.3.far_0_ref.refs_1_
  41.6 0.0 collective-permute-done.4.far_1_ref.refs_2_
  41.7 1.5 %collective-permute-start.10 = (bf16[2,512,256]{2,1,0:T(8,128)(2,1)S(1)}, bf16[2,512,256]{2,1,0:T(8,128)(2,1)S(1)}, u32[]{:S(2)}, u32[]{:S(2)}) collective-permute-start(bf16[2,512,256]{2,1,0:T(8,128)(2,1)S(1)} %shard_map.100.own_ref), channel_id=1, source_target_pairs={{0,16},{4,20},{8,24},{12,28},{16,0},{20,4},{24,8},{28,12},{1,17},{... | collective-permute-start | bytes 1572872 | tf_op jit(solution)/shard_map/ppermute | solution.py:224
  43.1 0.5 collective-permute-start.9
  43.7 1.1 %shard_map.97 = bf16[512,256]{1,0:T(8,128)(2,1)S(1)} custom-call(s32[2]{0:T(128)S(1)} %pad_add_fusion.me_ref.place_ref, bf16[256,1024]{1,0:T(8,128)(2,1)S(1)} %shard_map.94.x_ref, bf16[256,1024]{1,0:T(8,128)(2,1)S(1)} %collective-permute-done.y_ref, bf16[2,512,256]{2,1,0:T(8,128)(2,1)S(1)} %get-tuple-element.13.own_ref, ...), custom_call_target="tpu_custom_call" | custom-call | tf_op jit(solution)/shard_map/pallas_call | solution.py:245
  44.8 1.6 %collective-permute-start.5 = (bf16[512,256]{1,0:T(8,128)(2,1)S(1)}, bf16[512,256]{1,0:T(8,128)(2,1)S(1)}, u32[]{:S(2)}, u32[]{:S(2)}) collective-permute-start(bf16[512,256]{1,0:T(8,128)(2,1)S(1)} %shard_map.97), channel_id=1, source_target_pairs={{0,1},{1,0},{2,3},{3,2},{4,5},{5,4},{6,7},{7,6},{8,9},{9,8},{10,11... | collective-permute-start | bytes 786440 | tf_op jit(solution)/shard_map/ppermute | solution.py:224
  46.4 1.1 %shard_map.99 = bf16[512,256]{1,0:T(8,128)(2,1)S(1)} custom-call(s32[2]{0:T(128)S(1)} %pad_add_fusion.me_ref.place_ref, bf16[256,1024]{1,0:T(8,128)(2,1)S(1)} %shard_map.94.x_ref, bf16[256,1024]{1,0:T(8,128)(2,1)S(1)} %collective-permute-done.y_ref, bf16[2,512,256]{2,1,0:T(8,128)(2,1)S(1)} %get-tuple-element.13.own_ref, ...), custom_call_target="tpu_custom_call" | custom-call | tf_op jit(solution)/shard_map/pallas_call | solution.py:245
  47.5 0.5 collective-permute-start.6
  48.0 7.6 %collective-permute-done.10.refs_1_ = bf16[2,512,256]{2,1,0:T(8,128)(2,1)S(1)} collective-permute-done((bf16[2,512,256]{2,1,0:T(8,128)(2,1)S(1)}, bf16[2,512,256]{2,1,0:T(8,128)(2,1)S(1)}, u32[]{:S(2)}, u32[]{:S(2)}) %collective-permute-start.10) | collective-permute-done | bytes 524320 | tf_op jit(solution)/shard_map/ppermute | solution.py:224
  55.6 0.7 collective-permute-done.9.refs_0_
  56.3 0.0 collective-permute-done.5.refs_3_
  56.3 1.9 %collective-permute-done.6.refs_2_ = bf16[512,256]{1,0:T(8,128)(2,1)S(1)} collective-permute-done((bf16[512,256]{1,0:T(8,128)(2,1)S(1)}, bf16[512,256]{1,0:T(8,128)(2,1)S(1)}, u32[]{:S(2)}, u32[]{:S(2)}) %collective-permute-start.6) | collective-permute-done | bytes 262176 | tf_op jit(solution)/shard_map/ppermute | solution.py:224
  58.3 1.0 %collective-permute-start.11 = (bf16[1,512,256]{2,1,0:T(8,128)(2,1)S(1)}, bf16[1,512,256]{2,1,0:T(8,128)(2,1)S(1)}, u32[]{:S(2)}, u32[]{:S(2)}) collective-permute-start(bf16[1,512,256]{2,1,0:T(8,128)(2,1)S(1)} %slice.32), channel_id=1, source_target_pairs={{0,8},{4,12},{8,0},{12,4},{16,24},{20,28},{24,16},{28,20},{1,9},{5... | collective-permute-start | bytes 786440 | tf_op jit(solution)/shard_map/ppermute | solution.py:224
  59.3 1.0 %collective-permute-start.12 = (bf16[1,512,256]{2,1,0:T(8,128)(2,1)S(1)}, bf16[1,512,256]{2,1,0:T(8,128)(2,1)S(1)}, u32[]{:S(2)}, u32[]{:S(2)}) collective-permute-start(bf16[1,512,256]{2,1,0:T(8,128)(2,1)S(1)} %slice.33), channel_id=1, source_target_pairs={{0,16},{4,20},{8,24},{12,28},{16,0},{20,4},{24,8},{28,12},{1,17},{... | collective-permute-start | bytes 786440 | tf_op jit(solution)/shard_map/ppermute | solution.py:224
  60.3 4.9 %collective-permute-done.11.far_0_ref = bf16[1,512,256]{2,1,0:T(8,128)(2,1)S(1)} collective-permute-done((bf16[1,512,256]{2,1,0:T(8,128)(2,1)S(1)}, bf16[1,512,256]{2,1,0:T(8,128)(2,1)S(1)}, u32[]{:S(2)}, u32[]{:S(2)}) %collective-permute-start.11) | collective-permute-done | bytes 262176 | tf_op jit(solution)/shard_map/ppermute | solution.py:224
  65.3 0.4 collective-permute-done.12.far_1_ref
  65.7 1.1 %shard_map.105 = bf16[512,256]{1,0:T(8,128)(2,1)S(1)} custom-call(s32[2]{0:T(128)S(1)} %pad_add_fusion.me_ref.place_ref, bf16[256,1024]{1,0:T(8,128)(2,1)S(1)} %shard_map.94.x_ref, bf16[256,1024]{1,0:T(8,128)(2,1)S(1)} %collective-permute-done.y_ref, bf16[2,512,256]{2,1,0:T(8,128)(2,1)S(1)} %shard_map.100.own_ref, ...), custom_call_target="tpu_custom_call" | custom-call | tf_op jit(solution)/shard_map/pallas_call | solution.py:245
  66.8 1.6 %collective-permute-start.14 = (bf16[512,256]{1,0:T(8,128)(2,1)S(1)}, bf16[512,256]{1,0:T(8,128)(2,1)S(1)}, u32[]{:S(2)}, u32[]{:S(2)}) collective-permute-start(bf16[512,256]{1,0:T(8,128)(2,1)S(1)} %shard_map.105), channel_id=1, source_target_pairs={{0,1},{1,0},{2,3},{3,2},{4,5},{5,4},{6,7},{7,6},{8,9},{9,8},{10,11... | collective-permute-start | bytes 786440 | tf_op jit(solution)/shard_map/ppermute | solution.py:224
  68.4 1.1 %shard_map.98 = bf16[512,256]{1,0:T(8,128)(2,1)S(1)} custom-call(s32[2]{0:T(128)S(1)} %pad_add_fusion.me_ref.place_ref, bf16[256,1024]{1,0:T(8,128)(2,1)S(1)} %shard_map.94.x_ref, bf16[256,1024]{1,0:T(8,128)(2,1)S(1)} %collective-permute-done.y_ref, bf16[2,512,256]{2,1,0:T(8,128)(2,1)S(1)} %get-tuple-element.13.own_ref, ...), custom_call_target="tpu_custom_call" | custom-call | tf_op jit(solution)/shard_map/pallas_call | solution.py:245
  69.5 0.1 add_convert_fusion.3
  69.6 2.7 %collective-permute-start.7 = (bf16[512,256]{1,0:T(8,128)(2,1)S(1)}, bf16[512,256]{1,0:T(8,128)(2,1)S(1)}, u32[]{:S(2)}, u32[]{:S(2)}) collective-permute-start(bf16[512,256]{1,0:T(8,128)(2,1)S(1)} %add_convert_fusion.3), channel_id=1, source_target_pairs={{0,2},{1,3},{2,0},{3,1},{4,6},{5,7},{6,4},{7,5},{8,10},{9,11},{10,... | collective-permute-start | bytes 786440 | tf_op jit(solution)/shard_map/ppermute | solution.py:224
  72.2 1.1 %shard_map.96 = bf16[512,256]{1,0:T(8,128)(2,1)S(1)} custom-call(s32[2]{0:T(128)S(1)} %pad_add_fusion.me_ref.place_ref, bf16[256,1024]{1,0:T(8,128)(2,1)S(1)} %shard_map.94.x_ref, bf16[256,1024]{1,0:T(8,128)(2,1)S(1)} %collective-permute-done.y_ref, bf16[2,512,256]{2,1,0:T(8,128)(2,1)S(1)} %get-tuple-element.13.own_ref, ...), custom_call_target="tpu_custom_call" | custom-call | tf_op jit(solution)/shard_map/pallas_call | solution.py:245
  73.3 1.1 %shard_map.103 = bf16[512,256]{1,0:T(8,128)(2,1)S(1)} custom-call(s32[2]{0:T(128)S(1)} %pad_add_fusion.me_ref.place_ref, bf16[256,1024]{1,0:T(8,128)(2,1)S(1)} %shard_map.94.x_ref, bf16[256,1024]{1,0:T(8,128)(2,1)S(1)} %collective-permute-done.y_ref, bf16[2,512,256]{2,1,0:T(8,128)(2,1)S(1)} %shard_map.100.own_ref, ...), custom_call_target="tpu_custom_call" | custom-call | tf_op jit(solution)/shard_map/pallas_call | solution.py:245
  74.4 0.5 collective-permute-start.13
  74.9 1.1 %shard_map.104 = bf16[512,256]{1,0:T(8,128)(2,1)S(1)} custom-call(s32[2]{0:T(128)S(1)} %pad_add_fusion.me_ref.place_ref, bf16[256,1024]{1,0:T(8,128)(2,1)S(1)} %shard_map.94.x_ref, bf16[256,1024]{1,0:T(8,128)(2,1)S(1)} %collective-permute-done.y_ref, bf16[2,512,256]{2,1,0:T(8,128)(2,1)S(1)} %shard_map.100.own_ref, ...), custom_call_target="tpu_custom_call" | custom-call | tf_op jit(solution)/shard_map/pallas_call | solution.py:245
  76.0 4.4 %collective-permute-done.14 = bf16[512,256]{1,0:T(8,128)(2,1)S(1)} collective-permute-done((bf16[512,256]{1,0:T(8,128)(2,1)S(1)}, bf16[512,256]{1,0:T(8,128)(2,1)S(1)}, u32[]{:S(2)}, u32[]{:S(2)}) %collective-permute-start.14) | collective-permute-done | bytes 262176 | tf_op jit(solution)/shard_map/ppermute | solution.py:224
  80.4 0.1 add_convert_fusion.1
  80.5 2.8 %collective-permute-start.15 = (bf16[512,256]{1,0:T(8,128)(2,1)S(1)}, bf16[512,256]{1,0:T(8,128)(2,1)S(1)}, u32[]{:S(2)}, u32[]{:S(2)}) collective-permute-start(bf16[512,256]{1,0:T(8,128)(2,1)S(1)} %add_convert_fusion.1), channel_id=1, source_target_pairs={{0,2},{1,3},{2,0},{3,1},{4,6},{5,7},{6,4},{7,5},{8,10},{9,11},{10,... | collective-permute-start | bytes 786440 | tf_op jit(solution)/shard_map/ppermute | solution.py:224
  83.3 2.2 %collective-permute-done.7 = bf16[512,256]{1,0:T(8,128)(2,1)S(1)} collective-permute-done((bf16[512,256]{1,0:T(8,128)(2,1)S(1)}, bf16[512,256]{1,0:T(8,128)(2,1)S(1)}, u32[]{:S(2)}, u32[]{:S(2)}) %collective-permute-start.7) | collective-permute-done | bytes 262176 | tf_op jit(solution)/shard_map/ppermute | solution.py:224
  85.5 0.1 add_convert_fusion.2
  85.6 0.1 collective-permute-start.8
  85.7 1.1 %shard_map.102 = bf16[512,256]{1,0:T(8,128)(2,1)S(1)} custom-call(s32[2]{0:T(128)S(1)} %pad_add_fusion.me_ref.place_ref, bf16[256,1024]{1,0:T(8,128)(2,1)S(1)} %shard_map.94.x_ref, bf16[256,1024]{1,0:T(8,128)(2,1)S(1)} %collective-permute-done.y_ref, bf16[2,512,256]{2,1,0:T(8,128)(2,1)S(1)} %shard_map.100.own_ref, ...), custom_call_target="tpu_custom_call" | custom-call | tf_op jit(solution)/shard_map/pallas_call | solution.py:245
  86.8 0.7 collective-permute-done.13
  87.5 5.2 %collective-permute-done.15 = bf16[512,256]{1,0:T(8,128)(2,1)S(1)} collective-permute-done((bf16[512,256]{1,0:T(8,128)(2,1)S(1)}, bf16[512,256]{1,0:T(8,128)(2,1)S(1)}, u32[]{:S(2)}, u32[]{:S(2)}) %collective-permute-start.15) | collective-permute-done | bytes 262176 | tf_op jit(solution)/shard_map/ppermute | solution.py:224
  92.7 0.1 add_convert_fusion
  92.8 0.1 collective-permute-start.16
  92.9 1.3 %collective-permute-done.16.refs_3_ = bf16[256,256]{1,0:T(8,128)(2,1)S(1)} collective-permute-done((bf16[256,256]{1,0:T(8,128)(2,1)S(1)}, bf16[256,256]{1,0:T(8,128)(2,1)S(1)}, u32[]{:S(2)}, u32[]{:S(2)}) %collective-permute-start.16) | collective-permute-done | bytes 131104 | tf_op jit(solution)/shard_map/ppermute | solution.py:224
  94.2 1.4 %shard_map.106 = bf16[256,1024]{1,0:T(8,128)(2,1)} custom-call(s32[2]{0:T(128)S(1)} %pad_add_fusion.me_ref.place_ref, bf16[256,256]{1,0:T(8,128)(2,1)S(1)} %get-tuple-element.22.refs_0_, bf16[256,256]{1,0:T(8,128)(2,1)S(1)} %collective-permute-done.8.refs_1_, bf16[256,256]{1,0:T(8,128)(2,1)S(1)} %get-tuple-element.20.refs_2_, ...), custom_call_target="tpu_custom_call" | custom-call | tf_op jit(solution)/shard_map/pallas_call | solution.py:262
  (21 shorter events, 0.1 us)
Async XLA Ops:
  2.2 5.4 %copy-start = (bf16[1024,256]{1,0:T(8,128)(2,1)S(1)}, bf16[1024,256]{1,0:T(8,128)(2,1)}, u32[]{:S(2)}) copy-start(bf16[1024,256]{1,0:T(8,128)(2,1)} %shard_map.91.u_hbm) | copy-start | bytes 1572868
  2.2 5.4 %copy-start.5 = (f32[64,64]{1,0:T(8,128)S(1)}, f32[64,64]{1,0:T(8,128)}, u32[]{:S(2)}) copy-start(f32[64,64]{1,0:T(8,128)} %fout_hbm.1) | copy-start | bytes 49156
  2.2 5.4 %copy-start.9 = (f32[64]{0:T(128)S(1)}, f32[64]{0:T(128)}, u32[]{:S(2)}) copy-start(f32[64]{0:T(128)} %param.15) | copy-start | bytes 772
  2.2 15.5 %all-to-all-start = ((bf16[8,128,256]{2,1,0:T(8,128)(2,1)}), bf16[8,128,256]{2,1,0:T(8,128)(2,1)S(1)}, u32[]{:S(2)}, u32[]{:S(2)}) async-start(bf16[8,128,256]{2,1,0:T(8,128)(2,1)} %bitcast.7), calls=%async_computation | async-start | bytes 1048576 | tf_op jit(solution)/shard_map/all_to_all | solution.py:311
  7.5 0.7 copy-start.6
  7.6 0.7 copy-start.8
  8.3 1.2 %copy-start.3 = (bf16[1024,512]{1,0:T(8,128)(2,1)S(1)}, bf16[1024,512]{1,0:T(8,128)(2,1)}, u32[]{:S(2)}) copy-start(bf16[1024,512]{1,0:T(8,128)(2,1)} %w_hbm.1) | copy-start | bytes 3145732
  12.5 15.7 %collective-permute-start.2 = (bf16[2,512,256]{2,1,0:T(8,128)(2,1)S(1)}, bf16[2,512,256]{2,1,0:T(8,128)(2,1)S(1)}, u32[]{:S(2)}, u32[]{:S(2)}) collective-permute-start(bf16[2,512,256]{2,1,0:T(8,128)(2,1)S(1)} %get-tuple-element.13.own_ref), channel_id=1, source_target_pairs={{0,16},{4,20},{8,24},{12,28},{16,0},{20,4},{24,8},{28,12},{1,17},{... | collective-permute-start | bytes 1572872 | tf_op jit(solution)/shard_map/ppermute | solution.py:224
  14.6 13.7 %collective-permute-start.1 = (bf16[2,512,256]{2,1,0:T(8,128)(2,1)S(1)}, bf16[2,512,256]{2,1,0:T(8,128)(2,1)S(1)}, u32[]{:S(2)}, u32[]{:S(2)}) collective-permute-start(bf16[2,512,256]{2,1,0:T(8,128)(2,1)S(1)} %get-tuple-element.13.own_ref), channel_id=1, source_target_pairs={{0,8},{4,12},{8,0},{12,4},{16,24},{20,28},{24,16},{28,20},{1,9},{5... | collective-permute-start | bytes 1572872 | tf_op jit(solution)/shard_map/ppermute | solution.py:224
  23.1 14.4 %all-to-all-start.1 = ((bf16[8,128,256]{2,1,0:T(8,128)(2,1)}), bf16[8,128,256]{2,1,0:T(8,128)(2,1)}, u32[]{:S(2)}, u32[]{:S(2)}) async-start(bf16[8,128,256]{2,1,0:T(8,128)(2,1)} %shard_map.93.refs_2_), calls=%async_computation.1 | async-start | bytes 1048576 | tf_op jit(solution)/shard_map/all_to_all | solution.py:335
  28.3 9.3 %copy-start.1 = (bf16[256,1024]{1,0:T(8,128)(2,1)S(1)}, bf16[256,1024]{1,0:T(8,128)(2,1)}, u32[]{:S(2)}) copy-start(bf16[256,1024]{1,0:T(8,128)(2,1)} %k_hbm.3) | copy-start | bytes 1572868
  28.3 9.3 %copy-start.7 = (f32[1024]{0:T(1024)S(1)}, f32[1024]{0:T(1024)}, u32[]{:S(2)}) copy-start(f32[1024]{0:T(1024)} %param.16) | copy-start | bytes 12292
  29.0 12.6 %collective-permute-start.3 = (bf16[1,512,256]{2,1,0:T(8,128)(2,1)}, bf16[1,512,256]{2,1,0:T(8,128)(2,1)S(1)}, u32[]{:S(2)}, u32[]{:S(2)}) collective-permute-start(bf16[1,512,256]{2,1,0:T(8,128)(2,1)} %slice.28), channel_id=1, source_target_pairs={{0,8},{4,12},{8,0},{12,4},{16,24},{20,28},{24,16},{28,20},{1,9},{5... | collective-permute-start | bytes 786440 | tf_op jit(solution)/shard_map/ppermute | solution.py:224
  30.5 11.2 %collective-permute-start.4 = (bf16[1,512,256]{2,1,0:T(8,128)(2,1)S(1)}, bf16[1,512,256]{2,1,0:T(8,128)(2,1)S(1)}, u32[]{:S(2)}, u32[]{:S(2)}) collective-permute-start(bf16[1,512,256]{2,1,0:T(8,128)(2,1)S(1)} %slice.29), channel_id=1, source_target_pairs={{0,16},{4,20},{8,24},{12,28},{16,0},{20,4},{24,8},{28,12},{1,17},{... | collective-permute-start | bytes 786440 | tf_op jit(solution)/shard_map/ppermute | solution.py:224
  37.5 1.0 %copy-start.2 = (bf16[256,1024]{1,0:T(8,128)(2,1)S(1)}, bf16[256,1024]{1,0:T(8,128)(2,1)}, u32[]{:S(2)}) copy-start(bf16[256,1024]{1,0:T(8,128)(2,1)} %v_hbm.3) | copy-start | bytes 1572868
  38.6 1.0 %copy-start.4 = (bf16[256,1024]{1,0:T(8,128)(2,1)S(1)}, bf16[256,1024]{1,0:T(8,128)(2,1)}, u32[]{:S(2)}) copy-start(bf16[256,1024]{1,0:T(8,128)(2,1)} %q_hbm.1) | copy-start | bytes 1572868
  41.2 2.5 %collective-permute-start = (bf16[256,1024]{1,0:T(8,128)(2,1)S(1)}, bf16[256,1024]{1,0:T(8,128)(2,1)S(1)}, u32[]{:S(2)}, u32[]{:S(2)}) collective-permute-start(bf16[256,1024]{1,0:T(8,128)(2,1)S(1)} %shard_map.94.x_ref), channel_id=1, source_target_pairs={{0,4},{4,0},{8,12},{12,8},{16,20},{20,16},{24,28},{28,24},{1,5},{5... | collective-permute-start | bytes 1572872 | tf_op jit(solution)/shard_map/ppermute | solution.py:224
  41.7 13.9 %collective-permute-start.10 = (bf16[2,512,256]{2,1,0:T(8,128)(2,1)S(1)}, bf16[2,512,256]{2,1,0:T(8,128)(2,1)S(1)}, u32[]{:S(2)}, u32[]{:S(2)}) collective-permute-start(bf16[2,512,256]{2,1,0:T(8,128)(2,1)S(1)} %shard_map.100.own_ref), channel_id=1, source_target_pairs={{0,16},{4,20},{8,24},{12,28},{16,0},{20,4},{24,8},{28,12},{1,17},{... | collective-permute-start | bytes 1572872 | tf_op jit(solution)/shard_map/ppermute | solution.py:224
  43.1 13.2 %collective-permute-start.9 = (bf16[2,512,256]{2,1,0:T(8,128)(2,1)S(1)}, bf16[2,512,256]{2,1,0:T(8,128)(2,1)S(1)}, u32[]{:S(2)}, u32[]{:S(2)}) collective-permute-start(bf16[2,512,256]{2,1,0:T(8,128)(2,1)S(1)} %shard_map.100.own_ref), channel_id=1, source_target_pairs={{0,8},{4,12},{8,0},{12,4},{16,24},{20,28},{24,16},{28,20},{1,9},{5... | collective-permute-start | bytes 1572872 | tf_op jit(solution)/shard_map/ppermute | solution.py:224
  44.8 11.6 %collective-permute-start.5 = (bf16[512,256]{1,0:T(8,128)(2,1)S(1)}, bf16[512,256]{1,0:T(8,128)(2,1)S(1)}, u32[]{:S(2)}, u32[]{:S(2)}) collective-permute-start(bf16[512,256]{1,0:T(8,128)(2,1)S(1)} %shard_map.97), channel_id=1, source_target_pairs={{0,1},{1,0},{2,3},{3,2},{4,5},{5,4},{6,7},{7,6},{8,9},{9,8},{10,11... | collective-permute-start | bytes 786440 | tf_op jit(solution)/shard_map/ppermute | solution.py:224
  47.5 10.8 %collective-permute-start.6 = (bf16[512,256]{1,0:T(8,128)(2,1)S(1)}, bf16[512,256]{1,0:T(8,128)(2,1)S(1)}, u32[]{:S(2)}, u32[]{:S(2)}) collective-permute-start(bf16[512,256]{1,0:T(8,128)(2,1)S(1)} %shard_map.99), channel_id=1, source_target_pairs={{0,1},{1,0},{2,3},{3,2},{4,5},{5,4},{6,7},{7,6},{8,9},{9,8},{10,11... | collective-permute-start | bytes 786440 | tf_op jit(solution)/shard_map/ppermute | solution.py:224
  58.3 7.0 %collective-permute-start.11 = (bf16[1,512,256]{2,1,0:T(8,128)(2,1)S(1)}, bf16[1,512,256]{2,1,0:T(8,128)(2,1)S(1)}, u32[]{:S(2)}, u32[]{:S(2)}) collective-permute-start(bf16[1,512,256]{2,1,0:T(8,128)(2,1)S(1)} %slice.32), channel_id=1, source_target_pairs={{0,8},{4,12},{8,0},{12,4},{16,24},{20,28},{24,16},{28,20},{1,9},{5... | collective-permute-start | bytes 786440 | tf_op jit(solution)/shard_map/ppermute | solution.py:224
  59.3 6.4 %collective-permute-start.12 = (bf16[1,512,256]{2,1,0:T(8,128)(2,1)S(1)}, bf16[1,512,256]{2,1,0:T(8,128)(2,1)S(1)}, u32[]{:S(2)}, u32[]{:S(2)}) collective-permute-start(bf16[1,512,256]{2,1,0:T(8,128)(2,1)S(1)} %slice.33), channel_id=1, source_target_pairs={{0,16},{4,20},{8,24},{12,28},{16,0},{20,4},{24,8},{28,12},{1,17},{... | collective-permute-start | bytes 786440 | tf_op jit(solution)/shard_map/ppermute | solution.py:224
  66.8 13.6 %collective-permute-start.14 = (bf16[512,256]{1,0:T(8,128)(2,1)S(1)}, bf16[512,256]{1,0:T(8,128)(2,1)S(1)}, u32[]{:S(2)}, u32[]{:S(2)}) collective-permute-start(bf16[512,256]{1,0:T(8,128)(2,1)S(1)} %shard_map.105), channel_id=1, source_target_pairs={{0,1},{1,0},{2,3},{3,2},{4,5},{5,4},{6,7},{7,6},{8,9},{9,8},{10,11... | collective-permute-start | bytes 786440 | tf_op jit(solution)/shard_map/ppermute | solution.py:224
  69.6 15.9 %collective-permute-start.7 = (bf16[512,256]{1,0:T(8,128)(2,1)S(1)}, bf16[512,256]{1,0:T(8,128)(2,1)S(1)}, u32[]{:S(2)}, u32[]{:S(2)}) collective-permute-start(bf16[512,256]{1,0:T(8,128)(2,1)S(1)} %add_convert_fusion.3), channel_id=1, source_target_pairs={{0,2},{1,3},{2,0},{3,1},{4,6},{5,7},{6,4},{7,5},{8,10},{9,11},{10,... | collective-permute-start | bytes 786440 | tf_op jit(solution)/shard_map/ppermute | solution.py:224
  74.4 13.1 %collective-permute-start.13 = (bf16[512,256]{1,0:T(8,128)(2,1)S(1)}, bf16[512,256]{1,0:T(8,128)(2,1)S(1)}, u32[]{:S(2)}, u32[]{:S(2)}) collective-permute-start(bf16[512,256]{1,0:T(8,128)(2,1)S(1)} %shard_map.103), channel_id=1, source_target_pairs={{0,1},{1,0},{2,3},{3,2},{4,5},{5,4},{6,7},{7,6},{8,9},{9,8},{10,11... | collective-permute-start | bytes 786440 | tf_op jit(solution)/shard_map/ppermute | solution.py:224
  80.5 12.2 %collective-permute-start.15 = (bf16[512,256]{1,0:T(8,128)(2,1)S(1)}, bf16[512,256]{1,0:T(8,128)(2,1)S(1)}, u32[]{:S(2)}, u32[]{:S(2)}) collective-permute-start(bf16[512,256]{1,0:T(8,128)(2,1)S(1)} %add_convert_fusion.1), channel_id=1, source_target_pairs={{0,2},{1,3},{2,0},{3,1},{4,6},{5,7},{6,4},{7,5},{8,10},{9,11},{10,... | collective-permute-start | bytes 786440 | tf_op jit(solution)/shard_map/ppermute | solution.py:224
  85.6 7.3 %collective-permute-start.8 = (bf16[256,256]{1,0:T(8,128)(2,1)S(1)}, bf16[256,256]{1,0:T(8,128)(2,1)S(1)}, u32[]{:S(2)}, u32[]{:S(2)}) collective-permute-start(bf16[256,256]{1,0:T(8,128)(2,1)S(1)} %get-tuple-element.21), channel_id=1, source_target_pairs={{0,4},{4,0},{8,12},{12,8},{16,20},{20,16},{24,28},{28,24},{1,5},{5... | collective-permute-start | bytes 393224 | tf_op jit(solution)/shard_map/ppermute | solution.py:224
  92.8 1.4 %collective-permute-start.16 = (bf16[256,256]{1,0:T(8,128)(2,1)S(1)}, bf16[256,256]{1,0:T(8,128)(2,1)S(1)}, u32[]{:S(2)}, u32[]{:S(2)}) collective-permute-start(bf16[256,256]{1,0:T(8,128)(2,1)S(1)} %get-tuple-element.19), channel_id=1, source_target_pairs={{0,4},{4,0},{8,12},{12,8},{16,20},{20,16},{24,28},{28,24},{1,5},{5... | collective-permute-start | bytes 393224 | tf_op jit(solution)/shard_map/ppermute | solution.py:224

commit v3 on v2

--- a/solution.py
+++ b/solution.py
@@ -100,8 +100,11 @@
     fout = contract(pick, fout_ref[...], (((1,), (1,)), ((), ())))
     decay = jnp.sum(pick * decay_ref[...], axis=1, keepdims=True)
     raw = contract(fout, hidden, (((1,), (0,)), ((), ())))
-    o_ref[:, :LANE] = jnp.zeros((groups, LANE), F32)
-    o_ref[:, LANE:] = (raw * jnp.exp(-decay * time)).astype(BF).astype(F32)
+    taps = (raw * jnp.exp(-decay * time)).astype(BF).astype(F32)
+    for g in range(groups):
+        line = jnp.concatenate([jnp.zeros((1, LANE), F32), taps[g : g + 1, :]], 1)
+        line = jnp.broadcast_to(line, (SUB, LANE + seq))
+        o_ref[g] = pltpu.roll(line, 0, 1, stride=1, stride_axis=0).astype(BF)
     for move in moves:
         move.wait()
 
@@ -119,10 +122,9 @@
     rev[:, seq:] = jnp.zeros((rev.shape[0], rev.shape[1] - seq), BF)
     stores = []
     for g in range(groups):
-        line = jnp.broadcast_to(taps_ref[g : g + 1, :], (SUB, LANE + seq))
-        slab = pltpu.roll(line, 0, 1, stride=1, stride_axis=0)
+        slab = taps_ref[g]
         for k in range(LANE // SUB):
-            part = (slab if k == 0 else pltpu.roll(slab, SUB * k, 1)).astype(BF)
+            part = slab if k == 0 else pltpu.roll(slab, SUB * k, 1)
             for d in range(blocks):
                 toep[g % 2, LANE * d + SUB * k : LANE * d + SUB * (k + 1), :] = part[
                     :, LANE * (d + 1) : LANE * (d + 2)
@@ -146,23 +148,25 @@
         store.wait()
 
 
-def gate_kernel(q_hbm, k_hbm, v_hbm, skip_hbm, conv_hbm, o_ref, q_ref, k_ref, v_ref, skip_ref, conv_ref, sems):
+def gate_kernel(q_hbm, u_hbm, skip_hbm, conv_hbm, o_ref, q_ref, u_ref, skip_ref, conv_ref, sems):
     steps = sems.shape[0]
     part = q_hbm.shape[1] // steps
     spans = [slice(part * i, part * (i + 1)) for i in range(steps)]
-    pairs = ((q_hbm, q_ref), (k_hbm, k_ref), (v_hbm, v_ref), (skip_hbm, skip_ref))
     loads = []
     for i, at in enumerate(spans):
-        step = [pltpu.make_async_copy(conv_hbm.at[at], conv_ref.at[at], sems.at[i, 4])]
-        for n, (source, target) in enumerate(pairs):
-            step.append(pltpu.make_async_copy(source.at[:, at], target.at[:, at], sems.at[i, n]))
+        step = [
+            pltpu.make_async_copy(conv_hbm.at[at], conv_ref.at[at], sems.at[i, 0]),
+            pltpu.make_async_copy(u_hbm.at[at], u_ref.at[at], sems.at[i, 1]),
+            pltpu.make_async_copy(q_hbm.at[:, at], q_ref.at[:, at], sems.at[i, 2]),
+            pltpu.make_async_copy(skip_hbm.at[:, at], skip_ref.at[:, at], sems.at[i, 3]),
+        ]
         for load in step:
             load.start()
         loads.append(step)
     for i, at in enumerate(spans):
         for load in loads[i]:
             load.wait()
-        u = (k_ref[:, at].astype(F32) * v_ref[:, at].astype(F32)).astype(BF).astype(F32)
+        u = u_ref[at, :].astype(F32).T
         conv = conv_ref[at, :].astype(F32).T
         gated = q_ref[:, at].astype(F32) * (conv + skip_ref[:, at] * u)
         o_ref[:, at] = gated.astype(BF)
@@ -312,7 +316,7 @@
     small = (filter_in, filter_bias[None], filter_out, decay_rates[None])
     taps, *cuts = call(
         functools.partial(taps_kernel, seq),
-        out_shape=[shape((groups, LANE + seq), F32)]
+        out_shape=[shape((groups, SUB, LANE + seq), BF)]
         + [shape((2, depth // 2, n), BF) for n in chunks],
         in_specs=[SMEM] + [HBM] * 6,
         out_specs=[VMEM] + [HBM] * len(chunks),
@@ -336,15 +340,16 @@
     gated = call(
         gate_kernel,
         out_shape=shape((rows, channels), BF),
-        in_specs=[HBM] * 5,
+        in_specs=[HBM] * 4,
         out_specs=VMEM,
-        scratch_shapes=[pltpu.VMEM((rows, channels), BF)] * 3
-        + [
+        scratch_shapes=[
+            pltpu.VMEM((rows, channels), BF),
+            pltpu.VMEM((channels, rows), BF),
             pltpu.VMEM((1, channels), F32),
             pltpu.VMEM((channels, rows), BF),
-            DMA((steps, 5)),
+            DMA((steps, 4)),
         ],
-    )(query_proj, key_proj, value_proj, skip_gain[None], conv_t)
+    )(query_proj, u_t, skip_gain[None], conv_t)
     if pairs:
         return project_pairs(place, gated, cuts, conv_all)
     everything = lax.all_gather(out_weight, "ctx", axis=1, tiled=True)

time: 96.2 us -> 94.7 us (0.984)
  Pallas kernels: 22.1 us -> 20.6 us
    ppermute x17, waiting for transfers between devices: 30.9 us -> 33 us  [swap(): return lax.ppermute(value, axis, [(i, i ^ bit) for i in range(count)])]
    all_to_all x1, waiting for transfers between devices: 6.05 us -> 4.16 us  [local(): conv_t = lax.all_to_all(conv_all, 'ctx', 0, 0).reshape(channels, rows)]
    pallas_call x1, Pallas kernels: 5.43 us -> 3.58 us  [local(): call(functools.partial(conv_kernel, seq, width), out_shape=shape(u_all.sh...]
    all_to_all x1, waiting for transfers between devices: 1.67 us -> 0.47 us  [local(): u_all = lax.all_to_all(u_t.reshape(ctx_count, own, rows), 'ctx', 0, 0)]
  transfers between devices with their start and end apart: 19 -> 19, of which waited for: 15 -> 15; matrix products, arithmetic and copies ran while one was open for 1% -> 1% of each run, Pallas kernels for 18% -> 17%
where the time goes in v3:
time: 94.7 us; the launch traced here: 94.2 us
  waiting for transfers between devices  37.7 us (40%)
  starting transfers between devices  29.7 us (31%)
  Pallas kernels  20.6 us (22%)
  local copies, waits for them, and re-layouts  5.6 us (6%)
    ppermute x17, waiting for transfers between devices, swap(): return lax.ppermute(value, axis, [(i, i ^ bit) for i in range(count)])  33 us
    ppermute x17, starting transfers between devices, swap(): return lax.ppermute(value, axis, [(i, i ^ bit) for i in range(count)])  20.2 us
    pallas_call x8, Pallas kernels, project_pairs(): call(functools.partial(block_kernel, r), out_shape=shape((2 * rows, n), B...  8.52 us
    all_to_all x1, starting transfers between devices, local(): u_all = lax.all_to_all(u_t.reshape(ctx_count, own, rows), 'ctx', 0, 0)  5.31 us
    unnamed x20, local copies, waits for them, and re-layouts  4.79 us
    all_to_all x1, waiting for transfers between devices, local(): conv_t = lax.all_to_all(conv_all, 'ctx', 0, 0).reshape(channels, rows)  4.16 us
    all_to_all x1, starting transfers between devices, local(): conv_t = lax.all_to_all(conv_all, 'ctx', 0, 0).reshape(channels, rows)  4.16 us
    pallas_call x1, Pallas kernels, local(): call(functools.partial(conv_kernel, seq, width), out_shape=shape(u_all.sh...  3.58 us
  transfers between devices with their start and end apart: 19, of which 15 were waited for; matrix products, arithmetic and copies ran while one was open for 1% of the time, Pallas kernels for 17%

profile of v3, /device:TPU:0, one launch (start us, length us, event | category | flops | bytes accessed | tf_op | source)
XLA Modules:
  0.0 94.2 jit_solution(14801946063106833257)
XLA Ops:
  0.0 2.2 %shard_map.91.u_hbm = bf16[1024,256]{1,0:T(8,128)(2,1)} custom-call(bf16[256,1024]{1,0:T(8,128)(2,1)} %k_hbm.1, bf16[256,1024]{1,0:T(8,128)(2,1)} %v_hbm.1), custom_call_target="tpu_custom_call" | custom-call | tf_op jit(solution)/shard_map/pallas_call | solution.py:301
  2.2 0.0 copy-start
  2.2 0.0 copy-start.5
  2.2 0.0 copy-start.9
  2.2 5.3 %all-to-all-start = ((bf16[8,128,256]{2,1,0:T(8,128)(2,1)}), bf16[8,128,256]{2,1,0:T(8,128)(2,1)S(1)}, u32[]{:S(2)}, u32[]{:S(2)}) async-start(bf16[8,128,256]{2,1,0:T(8,128)(2,1)} %bitcast.7), calls=%async_computation | async-start | bytes 1048576 | tf_op jit(solution)/shard_map/all_to_all | solution.py:315
  7.6 0.1 pad_add_fusion.me_ref.place_ref
  7.6 0.6 copy-done.6
  8.3 0.0 copy-done.8
  8.3 1.2 %copy-done.1 = bf16[1024,512]{1,0:T(8,128)(2,1)S(1)} copy-done((bf16[1024,512]{1,0:T(8,128)(2,1)S(1)}, bf16[1024,512]{1,0:T(8,128)(2,1)}, u32[]{:S(2)}) %copy-start.1) | copy-done | bytes 1048600
  9.5 3.1 %shard_map.92 = (bf16[8,16,2176]{2,1,0:T(8,128)(2,1)S(1)}, bf16[2,512,256]{2,1,0:T(8,128)(2,1)S(1)}, bf16[2,512,256]{2,1,0:T(8,128)(2,1)S(1)}) custom-call(s32[2]{0:T(128)S(1)} %pad_add_fusion.me_ref.place_ref, f32[33,64]{1,0:T(8,128)S(1)} %copy-done.6, f32[1,64]{1,0:T(1,128)S(1)} %bitcast.9, f32[64,64]{1,0:T(8,128)S(1)} %copy-done.5, f32[1,64]{1,0:T(1,128)S(1)} %bitcast.10, ...), custom_call_target="tpu_custom_call" | custom-call | tf_op jit(solution)/shard_map/pallas_call | solution.py:317
  12.6 0.8 copy-done.2
  13.4 2.0 %collective-permute-start.2 = (bf16[2,512,256]{2,1,0:T(8,128)(2,1)S(1)}, bf16[2,512,256]{2,1,0:T(8,128)(2,1)S(1)}, u32[]{:S(2)}, u32[]{:S(2)}) collective-permute-start(bf16[2,512,256]{2,1,0:T(8,128)(2,1)S(1)} %get-tuple-element.13.own_ref), channel_id=1, source_target_pairs={{0,16},{4,20},{8,24},{12,28},{16,0},{20,4},{24,8},{28,12},{1,17},{... | collective-permute-start | bytes 1572872 | tf_op jit(solution)/shard_map/ppermute | solution.py:228
  15.4 1.5 %collective-permute-start.1 = (bf16[2,512,256]{2,1,0:T(8,128)(2,1)S(1)}, bf16[2,512,256]{2,1,0:T(8,128)(2,1)S(1)}, u32[]{:S(2)}, u32[]{:S(2)}) collective-permute-start(bf16[2,512,256]{2,1,0:T(8,128)(2,1)S(1)} %get-tuple-element.13.own_ref), channel_id=1, source_target_pairs={{0,8},{4,12},{8,0},{12,4},{16,24},{20,28},{24,16},{28,20},{1,9},{5... | collective-permute-start | bytes 1572872 | tf_op jit(solution)/shard_map/ppermute | solution.py:228
  16.9 0.5 all-to-all-done.u_hbm
  17.4 1.1 %copy-done.3 = bf16[8,16,2176]{2,1,0:T(8,128)(2,1)S(1)} copy-done((bf16[8,16,2176]{2,1,0:T(8,128)(2,1)S(1)}, bf16[8,16,2176]{2,1,0:T(8,128)(2,1)}, u32[]{:S(2)}) %copy-start.3) | copy-done | bytes 557080
  18.4 3.6 %shard_map.93.refs_2_ = bf16[8,128,256]{2,1,0:T(8,128)(2,1)} custom-call(bf16[8,16,2176]{2,1,0:T(8,128)(2,1)S(1)} %copy-done.3, bf16[8,128,256]{2,1,0:T(8,128)(2,1)S(1)} %all-to-all-done.u_hbm), custom_call_target="tpu_custom_call" | custom-call | tf_op jit(solution)/shard_map/pallas_call | solution.py:326
  22.0 4.2 %all-to-all-start.1 = ((bf16[8,128,256]{2,1,0:T(8,128)(2,1)}), bf16[8,128,256]{2,1,0:T(8,128)(2,1)}, u32[]{:S(2)}, u32[]{:S(2)}) async-start(bf16[8,128,256]{2,1,0:T(8,128)(2,1)} %shard_map.93.refs_2_), calls=%async_computation.1 | async-start | bytes 1048576 | tf_op jit(solution)/shard_map/all_to_all | solution.py:339
  26.2 2.3 %collective-permute-done.2.refs_1_ = bf16[2,512,256]{2,1,0:T(8,128)(2,1)S(1)} collective-permute-done((bf16[2,512,256]{2,1,0:T(8,128)(2,1)S(1)}, bf16[2,512,256]{2,1,0:T(8,128)(2,1)S(1)}, u32[]{:S(2)}, u32[]{:S(2)}) %collective-permute-start.2) | collective-permute-done | bytes 524320 | tf_op jit(solution)/shard_map/ppermute | solution.py:228
  28.5 0.6 collective-permute-done.1.refs_0_
  29.2 0.0 copy-start.7
  29.2 0.7 slice.28
  29.9 2.4 %collective-permute-start.3 = (bf16[1,512,256]{2,1,0:T(8,128)(2,1)}, bf16[1,512,256]{2,1,0:T(8,128)(2,1)S(1)}, u32[]{:S(2)}, u32[]{:S(2)}) collective-permute-start(bf16[1,512,256]{2,1,0:T(8,128)(2,1)} %slice.28), channel_id=1, source_target_pairs={{0,8},{4,12},{8,0},{12,4},{16,24},{20,28},{24,16},{28,20},{1,9},{5... | collective-permute-start | bytes 786440 | tf_op jit(solution)/shard_map/ppermute | solution.py:228
  32.2 0.0 collective-permute-start.4
  32.2 4.2 %all-to-all-done.1 = bf16[8,128,256]{2,1,0:T(8,128)(2,1)} async-done(((bf16[8,128,256]{2,1,0:T(8,128)(2,1)}), bf16[8,128,256]{2,1,0:T(8,128)(2,1)}, u32[]{:S(2)}, u32[]{:S(2)}) %all-to-all-start.1) | async-done | bytes 524320 | tf_op jit(solution)/shard_map/all_to_all | solution.py:339
  36.4 1.0 %copy-done.4 = bf16[256,1024]{1,0:T(8,128)(2,1)S(1)} copy-done((bf16[256,1024]{1,0:T(8,128)(2,1)S(1)}, bf16[256,1024]{1,0:T(8,128)(2,1)}, u32[]{:S(2)}) %copy-start.4) | copy-done | bytes 524312
  37.5 1.8 %shard_map.94.x_ref = bf16[256,1024]{1,0:T(8,128)(2,1)S(1)} custom-call(bf16[256,1024]{1,0:T(8,128)(2,1)S(1)} %copy-done.4, bf16[1024,256]{1,0:T(8,128)(2,1)S(1)} %copy-done, f32[1,1024]{1,0:T(1,128)S(1)} %bitcast.8, bf16[1024,256]{1,0:T(8,128)(2,1)} %bitcast.6.conv_hbm), custom_call_target="tpu_custom_call" | custom-call | tf_op jit(solution)/shard_map/pallas_call | solution.py:340
  39.2 0.1 collective-permute-start
  39.3 1.2 %collective-permute-done.3.far_0_ref.refs_1_ = bf16[1,512,256]{2,1,0:T(8,128)(2,1)S(1)} collective-permute-done((bf16[1,512,256]{2,1,0:T(8,128)(2,1)}, bf16[1,512,256]{2,1,0:T(8,128)(2,1)S(1)}, u32[]{:S(2)}, u32[]{:S(2)}) %collective-permute-start.3) | collective-permute-done | bytes 262176 | tf_op jit(solution)/shard_map/ppermute | solution.py:228
  40.5 0.0 collective-permute-done.4.far_1_ref.refs_2_
  40.5 1.5 %collective-permute-start.10 = (bf16[2,512,256]{2,1,0:T(8,128)(2,1)S(1)}, bf16[2,512,256]{2,1,0:T(8,128)(2,1)S(1)}, u32[]{:S(2)}, u32[]{:S(2)}) collective-permute-start(bf16[2,512,256]{2,1,0:T(8,128)(2,1)S(1)} %shard_map.100.own_ref), channel_id=1, source_target_pairs={{0,16},{4,20},{8,24},{12,28},{16,0},{20,4},{24,8},{28,12},{1,17},{... | collective-permute-start | bytes 1572872 | tf_op jit(solution)/shard_map/ppermute | solution.py:228
  42.0 0.5 collective-permute-start.9
  42.6 1.1 %shard_map.97 = bf16[512,256]{1,0:T(8,128)(2,1)S(1)} custom-call(s32[2]{0:T(128)S(1)} %pad_add_fusion.me_ref.place_ref, bf16[256,1024]{1,0:T(8,128)(2,1)S(1)} %shard_map.94.x_ref, bf16[256,1024]{1,0:T(8,128)(2,1)S(1)} %collective-permute-done.y_ref, bf16[2,512,256]{2,1,0:T(8,128)(2,1)S(1)} %get-tuple-element.13.own_ref, ...), custom_call_target="tpu_custom_call" | custom-call | tf_op jit(solution)/shard_map/pallas_call | solution.py:249
  43.6 1.6 %collective-permute-start.5 = (bf16[512,256]{1,0:T(8,128)(2,1)S(1)}, bf16[512,256]{1,0:T(8,128)(2,1)S(1)}, u32[]{:S(2)}, u32[]{:S(2)}) collective-permute-start(bf16[512,256]{1,0:T(8,128)(2,1)S(1)} %shard_map.97), channel_id=1, source_target_pairs={{0,1},{1,0},{2,3},{3,2},{4,5},{5,4},{6,7},{7,6},{8,9},{9,8},{10,11... | collective-permute-start | bytes 786440 | tf_op jit(solution)/shard_map/ppermute | solution.py:228
  45.3 1.1 %shard_map.99 = bf16[512,256]{1,0:T(8,128)(2,1)S(1)} custom-call(s32[2]{0:T(128)S(1)} %pad_add_fusion.me_ref.place_ref, bf16[256,1024]{1,0:T(8,128)(2,1)S(1)} %shard_map.94.x_ref, bf16[256,1024]{1,0:T(8,128)(2,1)S(1)} %collective-permute-done.y_ref, bf16[2,512,256]{2,1,0:T(8,128)(2,1)S(1)} %get-tuple-element.13.own_ref, ...), custom_call_target="tpu_custom_call" | custom-call | tf_op jit(solution)/shard_map/pallas_call | solution.py:249
  46.4 0.5 collective-permute-start.6
  46.9 7.1 %collective-permute-done.10.refs_1_ = bf16[2,512,256]{2,1,0:T(8,128)(2,1)S(1)} collective-permute-done((bf16[2,512,256]{2,1,0:T(8,128)(2,1)S(1)}, bf16[2,512,256]{2,1,0:T(8,128)(2,1)S(1)}, u32[]{:S(2)}, u32[]{:S(2)}) %collective-permute-start.10) | collective-permute-done | bytes 524320 | tf_op jit(solution)/shard_map/ppermute | solution.py:228
  54.0 1.2 %collective-permute-done.9.refs_0_ = bf16[2,512,256]{2,1,0:T(8,128)(2,1)S(1)} collective-permute-done((bf16[2,512,256]{2,1,0:T(8,128)(2,1)S(1)}, bf16[2,512,256]{2,1,0:T(8,128)(2,1)S(1)}, u32[]{:S(2)}, u32[]{:S(2)}) %collective-permute-start.9) | collective-permute-done | bytes 524320 | tf_op jit(solution)/shard_map/ppermute | solution.py:228
  55.2 1.6 %collective-permute-done.6.refs_2_ = bf16[512,256]{1,0:T(8,128)(2,1)S(1)} collective-permute-done((bf16[512,256]{1,0:T(8,128)(2,1)S(1)}, bf16[512,256]{1,0:T(8,128)(2,1)S(1)}, u32[]{:S(2)}, u32[]{:S(2)}) %collective-permute-start.6) | collective-permute-done | bytes 262176 | tf_op jit(solution)/shard_map/ppermute | solution.py:228
  56.8 1.4 %collective-permute-start.11 = (bf16[1,512,256]{2,1,0:T(8,128)(2,1)S(1)}, bf16[1,512,256]{2,1,0:T(8,128)(2,1)S(1)}, u32[]{:S(2)}, u32[]{:S(2)}) collective-permute-start(bf16[1,512,256]{2,1,0:T(8,128)(2,1)S(1)} %slice.32), channel_id=1, source_target_pairs={{0,8},{4,12},{8,0},{12,4},{16,24},{20,28},{24,16},{28,20},{1,9},{5... | collective-permute-start | bytes 786440 | tf_op jit(solution)/shard_map/ppermute | solution.py:228
  58.2 0.7 collective-permute-start.12
  58.9 4.5 %collective-permute-done.11.far_0_ref = bf16[1,512,256]{2,1,0:T(8,128)(2,1)S(1)} collective-permute-done((bf16[1,512,256]{2,1,0:T(8,128)(2,1)S(1)}, bf16[1,512,256]{2,1,0:T(8,128)(2,1)S(1)}, u32[]{:S(2)}, u32[]{:S(2)}) %collective-permute-start.11) | collective-permute-done | bytes 262176 | tf_op jit(solution)/shard_map/ppermute | solution.py:228
  63.4 1.2 %collective-permute-done.12.far_1_ref = bf16[1,512,256]{2,1,0:T(8,128)(2,1)S(1)} collective-permute-done((bf16[1,512,256]{2,1,0:T(8,128)(2,1)S(1)}, bf16[1,512,256]{2,1,0:T(8,128)(2,1)S(1)}, u32[]{:S(2)}, u32[]{:S(2)}) %collective-permute-start.12) | collective-permute-done | bytes 262176 | tf_op jit(solution)/shard_map/ppermute | solution.py:228
  64.6 1.1 %shard_map.105 = bf16[512,256]{1,0:T(8,128)(2,1)S(1)} custom-call(s32[2]{0:T(128)S(1)} %pad_add_fusion.me_ref.place_ref, bf16[256,1024]{1,0:T(8,128)(2,1)S(1)} %shard_map.94.x_ref, bf16[256,1024]{1,0:T(8,128)(2,1)S(1)} %collective-permute-done.y_ref, bf16[2,512,256]{2,1,0:T(8,128)(2,1)S(1)} %shard_map.100.own_ref, ...), custom_call_target="tpu_custom_call" | custom-call | tf_op jit(solution)/shard_map/pallas_call | solution.py:249
  65.6 1.6 %collective-permute-start.14 = (bf16[512,256]{1,0:T(8,128)(2,1)S(1)}, bf16[512,256]{1,0:T(8,128)(2,1)S(1)}, u32[]{:S(2)}, u32[]{:S(2)}) collective-permute-start(bf16[512,256]{1,0:T(8,128)(2,1)S(1)} %shard_map.105), channel_id=1, source_target_pairs={{0,1},{1,0},{2,3},{3,2},{4,5},{5,4},{6,7},{7,6},{8,9},{9,8},{10,11... | collective-permute-start | bytes 786440 | tf_op jit(solution)/shard_map/ppermute | solution.py:228
  67.3 1.1 %shard_map.98 = bf16[512,256]{1,0:T(8,128)(2,1)S(1)} custom-call(s32[2]{0:T(128)S(1)} %pad_add_fusion.me_ref.place_ref, bf16[256,1024]{1,0:T(8,128)(2,1)S(1)} %shard_map.94.x_ref, bf16[256,1024]{1,0:T(8,128)(2,1)S(1)} %collective-permute-done.y_ref, bf16[2,512,256]{2,1,0:T(8,128)(2,1)S(1)} %get-tuple-element.13.own_ref, ...), custom_call_target="tpu_custom_call" | custom-call | tf_op jit(solution)/shard_map/pallas_call | solution.py:249
  68.4 0.1 add_convert_fusion.3
  68.4 2.7 %collective-permute-start.7 = (bf16[512,256]{1,0:T(8,128)(2,1)S(1)}, bf16[512,256]{1,0:T(8,128)(2,1)S(1)}, u32[]{:S(2)}, u32[]{:S(2)}) collective-permute-start(bf16[512,256]{1,0:T(8,128)(2,1)S(1)} %add_convert_fusion.3), channel_id=1, source_target_pairs={{0,2},{1,3},{2,0},{3,1},{4,6},{5,7},{6,4},{7,5},{8,10},{9,11},{10,... | collective-permute-start | bytes 786440 | tf_op jit(solution)/shard_map/ppermute | solution.py:228
  71.1 1.1 %shard_map.96 = bf16[512,256]{1,0:T(8,128)(2,1)S(1)} custom-call(s32[2]{0:T(128)S(1)} %pad_add_fusion.me_ref.place_ref, bf16[256,1024]{1,0:T(8,128)(2,1)S(1)} %shard_map.94.x_ref, bf16[256,1024]{1,0:T(8,128)(2,1)S(1)} %collective-permute-done.y_ref, bf16[2,512,256]{2,1,0:T(8,128)(2,1)S(1)} %get-tuple-element.13.own_ref, ...), custom_call_target="tpu_custom_call" | custom-call | tf_op jit(solution)/shard_map/pallas_call | solution.py:249
  72.2 1.1 %shard_map.103 = bf16[512,256]{1,0:T(8,128)(2,1)S(1)} custom-call(s32[2]{0:T(128)S(1)} %pad_add_fusion.me_ref.place_ref, bf16[256,1024]{1,0:T(8,128)(2,1)S(1)} %shard_map.94.x_ref, bf16[256,1024]{1,0:T(8,128)(2,1)S(1)} %collective-permute-done.y_ref, bf16[2,512,256]{2,1,0:T(8,128)(2,1)S(1)} %shard_map.100.own_ref, ...), custom_call_target="tpu_custom_call" | custom-call | tf_op jit(solution)/shard_map/pallas_call | solution.py:249
  73.2 0.5 collective-permute-start.13
  73.8 1.1 %shard_map.104 = bf16[512,256]{1,0:T(8,128)(2,1)S(1)} custom-call(s32[2]{0:T(128)S(1)} %pad_add_fusion.me_ref.place_ref, bf16[256,1024]{1,0:T(8,128)(2,1)S(1)} %shard_map.94.x_ref, bf16[256,1024]{1,0:T(8,128)(2,1)S(1)} %collective-permute-done.y_ref, bf16[2,512,256]{2,1,0:T(8,128)(2,1)S(1)} %shard_map.100.own_ref, ...), custom_call_target="tpu_custom_call" | custom-call | tf_op jit(solution)/shard_map/pallas_call | solution.py:249
  74.8 4.3 %collective-permute-done.14 = bf16[512,256]{1,0:T(8,128)(2,1)S(1)} collective-permute-done((bf16[512,256]{1,0:T(8,128)(2,1)S(1)}, bf16[512,256]{1,0:T(8,128)(2,1)S(1)}, u32[]{:S(2)}, u32[]{:S(2)}) %collective-permute-start.14) | collective-permute-done | bytes 262176 | tf_op jit(solution)/shard_map/ppermute | solution.py:228
  79.1 0.1 add_convert_fusion.1
  79.2 3.1 %collective-permute-start.15 = (bf16[512,256]{1,0:T(8,128)(2,1)S(1)}, bf16[512,256]{1,0:T(8,128)(2,1)S(1)}, u32[]{:S(2)}, u32[]{:S(2)}) collective-permute-start(bf16[512,256]{1,0:T(8,128)(2,1)S(1)} %add_convert_fusion.1), channel_id=1, source_target_pairs={{0,2},{1,3},{2,0},{3,1},{4,6},{5,7},{6,4},{7,5},{8,10},{9,11},{10,... | collective-permute-start | bytes 786440 | tf_op jit(solution)/shard_map/ppermute | solution.py:228
  82.2 2.1 %collective-permute-done.7 = bf16[512,256]{1,0:T(8,128)(2,1)S(1)} collective-permute-done((bf16[512,256]{1,0:T(8,128)(2,1)S(1)}, bf16[512,256]{1,0:T(8,128)(2,1)S(1)}, u32[]{:S(2)}, u32[]{:S(2)}) %collective-permute-start.7) | collective-permute-done | bytes 262176 | tf_op jit(solution)/shard_map/ppermute | solution.py:228
  84.4 0.1 add_convert_fusion.2
  84.5 0.1 collective-permute-start.8
  84.6 1.1 %shard_map.102 = bf16[512,256]{1,0:T(8,128)(2,1)S(1)} custom-call(s32[2]{0:T(128)S(1)} %pad_add_fusion.me_ref.place_ref, bf16[256,1024]{1,0:T(8,128)(2,1)S(1)} %shard_map.94.x_ref, bf16[256,1024]{1,0:T(8,128)(2,1)S(1)} %collective-permute-done.y_ref, bf16[2,512,256]{2,1,0:T(8,128)(2,1)S(1)} %shard_map.100.own_ref, ...), custom_call_target="tpu_custom_call" | custom-call | tf_op jit(solution)/shard_map/pallas_call | solution.py:249
  85.7 0.2 collective-permute-done.13
  85.9 5.4 %collective-permute-done.15 = bf16[512,256]{1,0:T(8,128)(2,1)S(1)} collective-permute-done((bf16[512,256]{1,0:T(8,128)(2,1)S(1)}, bf16[512,256]{1,0:T(8,128)(2,1)S(1)}, u32[]{:S(2)}, u32[]{:S(2)}) %collective-permute-start.15) | collective-permute-done | bytes 262176 | tf_op jit(solution)/shard_map/ppermute | solution.py:228
  91.2 0.1 add_convert_fusion
  91.4 0.1 collective-permute-start.16
  91.5 1.3 %collective-permute-done.16.refs_3_ = bf16[256,256]{1,0:T(8,128)(2,1)S(1)} collective-permute-done((bf16[256,256]{1,0:T(8,128)(2,1)S(1)}, bf16[256,256]{1,0:T(8,128)(2,1)S(1)}, u32[]{:S(2)}, u32[]{:S(2)}) %collective-permute-start.16) | collective-permute-done | bytes 131104 | tf_op jit(solution)/shard_map/ppermute | solution.py:228
  92.8 1.4 %shard_map.106 = bf16[256,1024]{1,0:T(8,128)(2,1)} custom-call(s32[2]{0:T(128)S(1)} %pad_add_fusion.me_ref.place_ref, bf16[256,256]{1,0:T(8,128)(2,1)S(1)} %get-tuple-element.22.refs_0_, bf16[256,256]{1,0:T(8,128)(2,1)S(1)} %collective-permute-done.8.refs_1_, bf16[256,256]{1,0:T(8,128)(2,1)S(1)} %get-tuple-element.20.refs_2_, ...), custom_call_target="tpu_custom_call" | custom-call | tf_op jit(solution)/shard_map/pallas_call | solution.py:266
  (21 shorter events, 0.1 us)
Async XLA Ops:
  2.2 5.4 %copy-start = (bf16[1024,256]{1,0:T(8,128)(2,1)S(1)}, bf16[1024,256]{1,0:T(8,128)(2,1)}, u32[]{:S(2)}) copy-start(bf16[1024,256]{1,0:T(8,128)(2,1)} %shard_map.91.u_hbm) | copy-start | bytes 1572868
  2.2 5.4 %copy-start.5 = (f32[64,64]{1,0:T(8,128)S(1)}, f32[64,64]{1,0:T(8,128)}, u32[]{:S(2)}) copy-start(f32[64,64]{1,0:T(8,128)} %fout_hbm.1) | copy-start | bytes 49156
  2.2 5.4 %copy-start.9 = (f32[64]{0:T(128)S(1)}, f32[64]{0:T(128)}, u32[]{:S(2)}) copy-start(f32[64]{0:T(128)} %param.15) | copy-start | bytes 772
  2.2 15.1 %all-to-all-start = ((bf16[8,128,256]{2,1,0:T(8,128)(2,1)}), bf16[8,128,256]{2,1,0:T(8,128)(2,1)S(1)}, u32[]{:S(2)}, u32[]{:S(2)}) async-start(bf16[8,128,256]{2,1,0:T(8,128)(2,1)} %bitcast.7), calls=%async_computation | async-start | bytes 1048576 | tf_op jit(solution)/shard_map/all_to_all | solution.py:315
  7.5 0.7 copy-start.6
  7.6 0.7 copy-start.8
  8.3 1.2 %copy-start.1 = (bf16[1024,512]{1,0:T(8,128)(2,1)S(1)}, bf16[1024,512]{1,0:T(8,128)(2,1)}, u32[]{:S(2)}) copy-start(bf16[1024,512]{1,0:T(8,128)(2,1)} %w_hbm.1) | copy-start | bytes 3145732
  12.6 0.8 copy-start.2
  13.4 15.1 %collective-permute-start.2 = (bf16[2,512,256]{2,1,0:T(8,128)(2,1)S(1)}, bf16[2,512,256]{2,1,0:T(8,128)(2,1)S(1)}, u32[]{:S(2)}, u32[]{:S(2)}) collective-permute-start(bf16[2,512,256]{2,1,0:T(8,128)(2,1)S(1)} %get-tuple-element.13.own_ref), channel_id=1, source_target_pairs={{0,16},{4,20},{8,24},{12,28},{16,0},{20,4},{24,8},{28,12},{1,17},{... | collective-permute-start | bytes 1572872 | tf_op jit(solution)/shard_map/ppermute | solution.py:228
  15.4 13.7 %collective-permute-start.1 = (bf16[2,512,256]{2,1,0:T(8,128)(2,1)S(1)}, bf16[2,512,256]{2,1,0:T(8,128)(2,1)S(1)}, u32[]{:S(2)}, u32[]{:S(2)}) collective-permute-start(bf16[2,512,256]{2,1,0:T(8,128)(2,1)S(1)} %get-tuple-element.13.own_ref), channel_id=1, source_target_pairs={{0,8},{4,12},{8,0},{12,4},{16,24},{20,28},{24,16},{28,20},{1,9},{5... | collective-permute-start | bytes 1572872 | tf_op jit(solution)/shard_map/ppermute | solution.py:228
  17.4 1.1 %copy-start.3 = (bf16[8,16,2176]{2,1,0:T(8,128)(2,1)S(1)}, bf16[8,16,2176]{2,1,0:T(8,128)(2,1)}, u32[]{:S(2)}) copy-start(bf16[8,16,2176]{2,1,0:T(8,128)(2,1)} %copy-done.2) | copy-start | bytes 1671172
  22.0 14.4 %all-to-all-start.1 = ((bf16[8,128,256]{2,1,0:T(8,128)(2,1)}), bf16[8,128,256]{2,1,0:T(8,128)(2,1)}, u32[]{:S(2)}, u32[]{:S(2)}) async-start(bf16[8,128,256]{2,1,0:T(8,128)(2,1)} %shard_map.93.refs_2_), calls=%async_computation.1 | async-start | bytes 1048576 | tf_op jit(solution)/shard_map/all_to_all | solution.py:339
  29.2 7.3 %copy-start.7 = (f32[1024]{0:T(1024)S(1)}, f32[1024]{0:T(1024)}, u32[]{:S(2)}) copy-start(f32[1024]{0:T(1024)} %param.16) | copy-start | bytes 12292
  29.9 10.6 %collective-permute-start.3 = (bf16[1,512,256]{2,1,0:T(8,128)(2,1)}, bf16[1,512,256]{2,1,0:T(8,128)(2,1)S(1)}, u32[]{:S(2)}, u32[]{:S(2)}) collective-permute-start(bf16[1,512,256]{2,1,0:T(8,128)(2,1)} %slice.28), channel_id=1, source_target_pairs={{0,8},{4,12},{8,0},{12,4},{16,24},{20,28},{24,16},{28,20},{1,9},{5... | collective-permute-start | bytes 786440 | tf_op jit(solution)/shard_map/ppermute | solution.py:228
  32.2 8.3 %collective-permute-start.4 = (bf16[1,512,256]{2,1,0:T(8,128)(2,1)S(1)}, bf16[1,512,256]{2,1,0:T(8,128)(2,1)S(1)}, u32[]{:S(2)}, u32[]{:S(2)}) collective-permute-start(bf16[1,512,256]{2,1,0:T(8,128)(2,1)S(1)} %slice.29), channel_id=1, source_target_pairs={{0,16},{4,20},{8,24},{12,28},{16,0},{20,4},{24,8},{28,12},{1,17},{... | collective-permute-start | bytes 786440 | tf_op jit(solution)/shard_map/ppermute | solution.py:228
  36.4 1.0 %copy-start.4 = (bf16[256,1024]{1,0:T(8,128)(2,1)S(1)}, bf16[256,1024]{1,0:T(8,128)(2,1)}, u32[]{:S(2)}) copy-start(bf16[256,1024]{1,0:T(8,128)(2,1)} %q_hbm.1) | copy-start | bytes 1572868
  39.2 3.3 %collective-permute-start = (bf16[256,1024]{1,0:T(8,128)(2,1)S(1)}, bf16[256,1024]{1,0:T(8,128)(2,1)S(1)}, u32[]{:S(2)}, u32[]{:S(2)}) collective-permute-start(bf16[256,1024]{1,0:T(8,128)(2,1)S(1)} %shard_map.94.x_ref), channel_id=1, source_target_pairs={{0,4},{4,0},{8,12},{12,8},{16,20},{20,16},{24,28},{28,24},{1,5},{5... | collective-permute-start | bytes 1572872 | tf_op jit(solution)/shard_map/ppermute | solution.py:228
  40.5 13.5 %collective-permute-start.10 = (bf16[2,512,256]{2,1,0:T(8,128)(2,1)S(1)}, bf16[2,512,256]{2,1,0:T(8,128)(2,1)S(1)}, u32[]{:S(2)}, u32[]{:S(2)}) collective-permute-start(bf16[2,512,256]{2,1,0:T(8,128)(2,1)S(1)} %shard_map.100.own_ref), channel_id=1, source_target_pairs={{0,16},{4,20},{8,24},{12,28},{16,0},{20,4},{24,8},{28,12},{1,17},{... | collective-permute-start | bytes 1572872 | tf_op jit(solution)/shard_map/ppermute | solution.py:228
  42.0 13.2 %collective-permute-start.9 = (bf16[2,512,256]{2,1,0:T(8,128)(2,1)S(1)}, bf16[2,512,256]{2,1,0:T(8,128)(2,1)S(1)}, u32[]{:S(2)}, u32[]{:S(2)}) collective-permute-start(bf16[2,512,256]{2,1,0:T(8,128)(2,1)S(1)} %shard_map.100.own_ref), channel_id=1, source_target_pairs={{0,8},{4,12},{8,0},{12,4},{16,24},{20,28},{24,16},{28,20},{1,9},{5... | collective-permute-start | bytes 1572872 | tf_op jit(solution)/shard_map/ppermute | solution.py:228
  43.6 11.6 %collective-permute-start.5 = (bf16[512,256]{1,0:T(8,128)(2,1)S(1)}, bf16[512,256]{1,0:T(8,128)(2,1)S(1)}, u32[]{:S(2)}, u32[]{:S(2)}) collective-permute-start(bf16[512,256]{1,0:T(8,128)(2,1)S(1)} %shard_map.97), channel_id=1, source_target_pairs={{0,1},{1,0},{2,3},{3,2},{4,5},{5,4},{6,7},{7,6},{8,9},{9,8},{10,11... | collective-permute-start | bytes 786440 | tf_op jit(solution)/shard_map/ppermute | solution.py:228
  46.4 10.4 %collective-permute-start.6 = (bf16[512,256]{1,0:T(8,128)(2,1)S(1)}, bf16[512,256]{1,0:T(8,128)(2,1)S(1)}, u32[]{:S(2)}, u32[]{:S(2)}) collective-permute-start(bf16[512,256]{1,0:T(8,128)(2,1)S(1)} %shard_map.99), channel_id=1, source_target_pairs={{0,1},{1,0},{2,3},{3,2},{4,5},{5,4},{6,7},{7,6},{8,9},{9,8},{10,11... | collective-permute-start | bytes 786440 | tf_op jit(solution)/shard_map/ppermute | solution.py:228
  56.8 6.6 %collective-permute-start.11 = (bf16[1,512,256]{2,1,0:T(8,128)(2,1)S(1)}, bf16[1,512,256]{2,1,0:T(8,128)(2,1)S(1)}, u32[]{:S(2)}, u32[]{:S(2)}) collective-permute-start(bf16[1,512,256]{2,1,0:T(8,128)(2,1)S(1)} %slice.32), channel_id=1, source_target_pairs={{0,8},{4,12},{8,0},{12,4},{16,24},{20,28},{24,16},{28,20},{1,9},{5... | collective-permute-start | bytes 786440 | tf_op jit(solution)/shard_map/ppermute | solution.py:228
  58.2 6.4 %collective-permute-start.12 = (bf16[1,512,256]{2,1,0:T(8,128)(2,1)S(1)}, bf16[1,512,256]{2,1,0:T(8,128)(2,1)S(1)}, u32[]{:S(2)}, u32[]{:S(2)}) collective-permute-start(bf16[1,512,256]{2,1,0:T(8,128)(2,1)S(1)} %slice.33), channel_id=1, source_target_pairs={{0,16},{4,20},{8,24},{12,28},{16,0},{20,4},{24,8},{28,12},{1,17},{... | collective-permute-start | bytes 786440 | tf_op jit(solution)/shard_map/ppermute | solution.py:228
  65.6 13.5 %collective-permute-start.14 = (bf16[512,256]{1,0:T(8,128)(2,1)S(1)}, bf16[512,256]{1,0:T(8,128)(2,1)S(1)}, u32[]{:S(2)}, u32[]{:S(2)}) collective-permute-start(bf16[512,256]{1,0:T(8,128)(2,1)S(1)} %shard_map.105), channel_id=1, source_target_pairs={{0,1},{1,0},{2,3},{3,2},{4,5},{5,4},{6,7},{7,6},{8,9},{9,8},{10,11... | collective-permute-start | bytes 786440 | tf_op jit(solution)/shard_map/ppermute | solution.py:228
  68.4 15.9 %collective-permute-start.7 = (bf16[512,256]{1,0:T(8,128)(2,1)S(1)}, bf16[512,256]{1,0:T(8,128)(2,1)S(1)}, u32[]{:S(2)}, u32[]{:S(2)}) collective-permute-start(bf16[512,256]{1,0:T(8,128)(2,1)S(1)} %add_convert_fusion.3), channel_id=1, source_target_pairs={{0,2},{1,3},{2,0},{3,1},{4,6},{5,7},{6,4},{7,5},{8,10},{9,11},{10,... | collective-permute-start | bytes 786440 | tf_op jit(solution)/shard_map/ppermute | solution.py:228
  73.2 12.6 %collective-permute-start.13 = (bf16[512,256]{1,0:T(8,128)(2,1)S(1)}, bf16[512,256]{1,0:T(8,128)(2,1)S(1)}, u32[]{:S(2)}, u32[]{:S(2)}) collective-permute-start(bf16[512,256]{1,0:T(8,128)(2,1)S(1)} %shard_map.103), channel_id=1, source_target_pairs={{0,1},{1,0},{2,3},{3,2},{4,5},{5,4},{6,7},{7,6},{8,9},{9,8},{10,11... | collective-permute-start | bytes 786440 | tf_op jit(solution)/shard_map/ppermute | solution.py:228
  79.2 12.0 %collective-permute-start.15 = (bf16[512,256]{1,0:T(8,128)(2,1)S(1)}, bf16[512,256]{1,0:T(8,128)(2,1)S(1)}, u32[]{:S(2)}, u32[]{:S(2)}) collective-permute-start(bf16[512,256]{1,0:T(8,128)(2,1)S(1)} %add_convert_fusion.1), channel_id=1, source_target_pairs={{0,2},{1,3},{2,0},{3,1},{4,6},{5,7},{6,4},{7,5},{8,10},{9,11},{10,... | collective-permute-start | bytes 786440 | tf_op jit(solution)/shard_map/ppermute | solution.py:228
  84.5 6.9 %collective-permute-start.8 = (bf16[256,256]{1,0:T(8,128)(2,1)S(1)}, bf16[256,256]{1,0:T(8,128)(2,1)S(1)}, u32[]{:S(2)}, u32[]{:S(2)}) collective-permute-start(bf16[256,256]{1,0:T(8,128)(2,1)S(1)} %get-tuple-element.21), channel_id=1, source_target_pairs={{0,4},{4,0},{8,12},{12,8},{16,20},{20,16},{24,28},{28,24},{1,5},{5... | collective-permute-start | bytes 393224 | tf_op jit(solution)/shard_map/ppermute | solution.py:228
  91.4 1.4 %collective-permute-start.16 = (bf16[256,256]{1,0:T(8,128)(2,1)S(1)}, bf16[256,256]{1,0:T(8,128)(2,1)S(1)}, u32[]{:S(2)}, u32[]{:S(2)}) collective-permute-start(bf16[256,256]{1,0:T(8,128)(2,1)S(1)} %get-tuple-element.19), channel_id=1, source_target_pairs={{0,4},{4,0},{8,12},{12,8},{16,20},{20,16},{24,28},{28,24},{1,5},{5... | collective-permute-start | bytes 393224 | tf_op jit(solution)/shard_map/ppermute | solution.py:228
